TPU v7x, 512 devices: a whole 4x8x8 slice. The times are simulated.
512 devices in a mesh: clip: 16 (over x_hi, y), tm: 32 (over z, x_lo, core).
Axes of the slice: x: 4 (x_hi: 2, x_lo: 2; x = x_hi * 2 + x_lo), y: 8, z: 8, core: 2. Of those that a mesh axis runs over, the one named last changes fastest.
Arguments:
- video: bfloat16 [16, 64, 288, 384], P('clip', 'tm'), may hold values from -6 to 6
- conv_w: bfloat16 [3, 384, 384], P(None, 'tm'), may hold values from -0.1875 to 0.1875
- qkv_w: bfloat16 [384, 1152], P('tm'), as said below
- out_w: bfloat16 [384, 384], P('tm'), may hold values from -0.3125 to 0.3125
- gain: bfloat16 [384], P('tm'), may hold values from 0.5 to 3.5
- cotangent: bfloat16 [16, 64, 288, 384], P('clip', 'tm'), may hold values from -6 to 6
Outputs:
- grad_video: bfloat16 [16, 64, 288, 384], P('clip', 'tm')
- grad_conv: float32 [3, 384, 384], P(None, 'tm')
- grad_qkv: float32 [384, 1152], P('tm')
- grad_out: float32 [384, 384], P('tm')
- grad_gain: float32 [384], P('tm')
Inputs may be any that keep to these rules, and one draw needn't show every extreme that they name: `qkv_w`: projection weights with entries of order 384^-0.5.
All inputs are finite; a program needn't handle non-finite values.
Results may differ from a plain program's by a relative error of at most 0.035.
Values may be sent and summed in bfloat16 or wider, within the bound.
A program may use at most 64 MiB of HBM per device.

v0:
```python
import math

import jax
import jax.numpy as jnp
from jax import lax
from jax.sharding import PartitionSpec as P

epsilon = 1e-06


def passed_along(x, axis, by):
    size = lax.axis_size(axis)
    pairs = [(i, i + by) for i in range(size) if 0 <= i + by < size]
    return lax.ppermute(x, axis, pairs)


def project(values, matrix):
    flat = values.reshape(-1, values.shape[-1])
    product = jnp.dot(flat, matrix, preferred_element_type=jnp.float32)
    return product.reshape(values.shape[:-1] + (matrix.shape[-1],))


def weight_grad(left, right):
    flat_left = left.reshape(-1, left.shape[-1])
    flat_right = right.reshape(-1, right.shape[-1])
    return lax.dot_general(
        flat_left, flat_right, (((0,), (0,)), ((), ())), preferred_element_type=jnp.float32
    )


def normalize(hidden, gain):
    wide = hidden.astype(jnp.float32)
    inverse = lax.rsqrt(jnp.mean(wide * wide, axis=-1, keepdims=True) + epsilon)
    return ((wide * inverse * gain.astype(jnp.float32)).astype(jnp.bfloat16), inverse)


def normalize_back(hidden, inverse, gain, grad_norm, cotangent):
    wide = hidden.astype(jnp.float32)
    incoming = grad_norm.astype(jnp.float32)
    scaled = incoming * gain.astype(jnp.float32)
    inner = jnp.mean(scaled * wide, axis=-1, keepdims=True)
    grad_hidden = cotangent.astype(jnp.float32) + inverse * scaled - wide * inverse**3 * inner
    gain_terms = jnp.sum((incoming * wide * inverse).reshape(-1, wide.shape[-1]), axis=0)
    return (grad_hidden.astype(jnp.bfloat16), gain_terms)


def attend(query, keys, values):
    factor = 1.0 / math.sqrt(query.shape[-1])
    scores = jnp.einsum("tpc,upc->ptu", query, keys, preferred_element_type=jnp.float32) * factor
    length = query.shape[0]
    causal = jnp.arange(length)[:, None] >= jnp.arange(length)[None, :]
    scores = jnp.where(causal[None], scores, -1e30)
    top = jnp.max(scores, axis=-1, keepdims=True)
    raised = jnp.exp(scores - top)
    probs = raised / jnp.sum(raised, axis=-1, keepdims=True)
    rounded = probs.astype(jnp.bfloat16)
    attended = jnp.einsum("ptu,upc->tpc", rounded, values, preferred_element_type=jnp.float32)
    return (attended.astype(jnp.bfloat16), probs, rounded)


def attend_back(query, keys, values, probs, rounded, grad_att):
    factor = 1.0 / math.sqrt(query.shape[-1])
    dprob = jnp.einsum("tpc,upc->ptu", grad_att, values, preferred_element_type=jnp.float32)
    dvalue = jnp.einsum("ptu,tpc->upc", rounded, grad_att, preferred_element_type=jnp.float32)
    dscore = probs * (dprob - jnp.sum(dprob * probs, axis=-1, keepdims=True))
    dquery = (
        jnp.einsum(
            "ptu,upc->tpc", dscore, keys.astype(jnp.float32), precision=lax.Precision.HIGHEST
        )
        * factor
    )
    dkey = (
        jnp.einsum(
            "ptu,tpc->upc", dscore, query.astype(jnp.float32), precision=lax.Precision.HIGHEST
        )
        * factor
    )
    return jnp.concatenate(
        [dquery.astype(jnp.bfloat16), dkey.astype(jnp.bfloat16), dvalue.astype(jnp.bfloat16)], -1
    )


def conv_forward(frames, extended, conv_full, gain_full):
    count = frames.shape[0]
    taps = [extended[2:], extended[1 : count + 1], extended[:count]]
    mixed = (
        project(taps[0], conv_full[0])
        + project(taps[1], conv_full[1])
        + project(taps[2], conv_full[2])
    )
    hidden = (frames.astype(jnp.float32) + mixed).astype(jnp.bfloat16)
    normed, inverse = normalize(hidden, gain_full)
    return (taps, hidden, normed, inverse)


def conv_backward(grad_hidden, grad_ext, taps, conv_full):
    count = grad_hidden.shape[0]
    grad_frames = grad_hidden.astype(jnp.float32) + project(grad_ext[:count], conv_full[0].T)
    grad_frames = grad_frames + project(grad_ext[1 : count + 1], conv_full[1].T)
    grad_frames = grad_frames + project(grad_ext[2:], conv_full[2].T)
    conv_part = jnp.stack(
        [
            weight_grad(taps[0], grad_hidden),
            weight_grad(taps[1], grad_hidden),
            weight_grad(taps[2], grad_hidden),
        ],
        0,
    )
    return (grad_frames.astype(jnp.bfloat16), conv_part)


def body(video, conv_w, qkv_w, out_w, gain, cotangent):
    conv_full, qkv_full, out_full, gain_full = (
        lax.all_gather(conv_w, "tm", axis=1, tiled=True),
        lax.all_gather(qkv_w, "tm", axis=0, tiled=True),
        lax.all_gather(out_w, "tm", axis=0, tiled=True),
        lax.all_gather(gain, "tm", axis=0, tiled=True),
    )
    width = video.shape[3]
    frames = video[0]
    count = frames.shape[0]
    past = passed_along(frames, "tm", 1)
    extended = jnp.concatenate([past, frames], 0)
    taps, hidden, normed, inverse = conv_forward(frames, extended, conv_full, gain_full)
    packed = project(normed, qkv_full).astype(jnp.bfloat16)
    spread = lax.all_to_all(packed, "tm", split_axis=1, concat_axis=0, tiled=True)
    query = spread[..., :width]
    keys = spread[..., width : 2 * width]
    values = spread[..., 2 * width :]
    attended, probs, rounded = attend(query, keys, values)
    attended_local = lax.all_to_all(attended, "tm", split_axis=0, concat_axis=1, tiled=True)
    grad_output = cotangent[0]
    grad_att = project(grad_output, out_full.T).astype(jnp.bfloat16)
    out_part = weight_grad(attended_local, grad_output)
    grad_spread = lax.all_to_all(grad_att, "tm", split_axis=1, concat_axis=0, tiled=True)
    grad_packed = attend_back(query, keys, values, probs, rounded, grad_spread)
    grad_back = lax.all_to_all(grad_packed, "tm", split_axis=0, concat_axis=1, tiled=True)
    qkv_part = weight_grad(normed, grad_back)
    grad_norm = project(grad_back, qkv_full.T).astype(jnp.bfloat16)
    grad_hidden, gain_part = normalize_back(hidden, inverse, gain_full, grad_norm, grad_output)
    later = passed_along(grad_hidden, "tm", -1)
    grad_ext = jnp.concatenate([grad_hidden, later], 0)
    grad_local, conv_part = conv_backward(grad_hidden, grad_ext, taps, conv_full)
    shards = (
        lax.psum_scatter(
            conv_part.astype(jnp.bfloat16), "tm", scatter_dimension=1, tiled=True
        ).astype(jnp.float32),
        lax.psum_scatter(
            qkv_part.astype(jnp.bfloat16), "tm", scatter_dimension=0, tiled=True
        ).astype(jnp.float32),
        lax.psum_scatter(
            out_part.astype(jnp.bfloat16), "tm", scatter_dimension=0, tiled=True
        ).astype(jnp.float32),
        lax.psum_scatter(
            gain_part.astype(jnp.bfloat16), "tm", scatter_dimension=0, tiled=True
        ).astype(jnp.float32),
    )
    totals = (
        lax.psum(shards[0].astype(jnp.bfloat16), "clip").astype(jnp.float32),
        lax.psum(shards[1].astype(jnp.bfloat16), "clip").astype(jnp.float32),
        lax.psum(shards[2].astype(jnp.bfloat16), "clip").astype(jnp.float32),
        lax.psum(shards[3].astype(jnp.bfloat16), "clip").astype(jnp.float32),
    )
    factor = 1.0 / math.sqrt(
        lax.axis_size("clip") * lax.axis_size("tm") * video.shape[1] * video.shape[2]
    )
    return (
        grad_local[None],
        totals[0] * factor,
        totals[1] * factor,
        totals[2] * factor,
        totals[3] * factor,
    )


def solution(mesh):
    in_specs = (
        P("clip", "tm", None, None),
        P(None, "tm", None),
        P("tm", None),
        P("tm", None),
        P("tm"),
        P("clip", "tm", None, None),
    )
    out_specs = (
        P("clip", "tm", None, None),
        P(None, "tm", None),
        P("tm", None),
        P("tm", None),
        P("tm"),
    )
    return jax.shard_map(body, mesh=mesh, in_specs=in_specs, out_specs=out_specs, check_vma=False)
```

profile of v0, /device:TPU:1, one launch (start us, length us, event | category | flops | bytes accessed | tf_op | source)
XLA Modules:
  0.0 738.3 jit_solution(18209139374081622353)
XLA Ops:
  7.2 43.0 %all-gather.1 = bf16[32,12,384]{2,1,0:T(8,128)(2,1)S(1)} all-gather(bf16[1,12,384]{2,1,0:T(8,128)(2,1)} %bitcast.128), channel_id=1, replica_groups=mesh['clip'=16,'tm'=32] {'tm'}, dimensions={0}, use_global_device_ids=true | all-gather | bytes 304128 | tf_op jit(solution)/shard_map/all_gather | solution.py:116
  52.9 3.7 all-to-all-start.1
  56.6 3.5 collective-permute-start
  60.2 41.5 %all_gather.12 = bf16[3,384,384]{2,0,1:T(4,128)(2,1)S(1)} all-gather(bf16[3,12,384]{2,0,1:T(4,128)(2,1)S(1)} %copy.30), channel_id=1, replica_groups=mesh['clip'=16,'tm'=32] {'tm'}, dimensions={1}, use_global_device_ids=true | all-gather | bytes 912384 | tf_op jit(solution)/shard_map/all_gather | solution.py:114
  101.7 33.9 %all-gather = bf16[32,12,1152]{2,1,0:T(8,128)(2,1)S(1)} all-gather(bf16[1,12,1152]{2,1,0:T(8,128)(2,1)S(1)} %bitcast.127), channel_id=1, replica_groups=mesh['clip'=16,'tm'=32] {'tm'}, dimensions={0}, use_global_device_ids=true | all-gather | bytes 912384 | tf_op jit(solution)/shard_map/all_gather | solution.py:115
  139.5 52.6 %all-reduce = bf16[384]{0:T(512)(128)(2,1)S(1)} all-reduce(bf16[384]{0:T(512)(128)(2,1)S(1)} %dynamic-update-slice), channel_id=1, replica_groups=mesh['clip'=16,'tm'=32] {'tm'}, use_global_device_ids=true, to_apply=%add | all-reduce | flops 384 | bytes 1536
  200.4 9.0 %all-to-all-start = ((bf16[2,288,1152]{2,0,1:T(2,128)(2,1)}), bf16[2,288,1152]{2,0,1:T(2,128)(2,1)S(1)}, u32[]{:S(2)}, u32[]{:S(2)}) async-start(bf16[2,288,1152]{2,0,1:T(2,128)(2,1)} %copy.34), calls=%async_computation | async-start | bytes 2654208 | tf_op jit(solution)/shard_map/all_to_all | solution.py:126
  211.2 32.2 %all-to-all-done = bf16[2,288,1152]{2,0,1:T(2,128)(2,1)S(1)} async-done(((bf16[2,288,1152]{2,0,1:T(2,128)(2,1)}), bf16[2,288,1152]{2,0,1:T(2,128)(2,1)S(1)}, u32[]{:S(2)}, u32[]{:S(2)}) %all-to-all-start) | async-done | bytes 1327136 | tf_op jit(solution)/shard_map/all_to_all | solution.py:126
  248.4 4.5 all-to-all-start.3
  262.0 13.0 %all-to-all-done.3 = bf16[64,9,384]{2,1,0:T(8,128)(2,1)S(1)} async-done(((bf16[64,9,384]{2,1,0:T(8,128)(2,1)}), bf16[64,9,384]{2,1,0:T(8,128)(2,1)S(1)}, u32[]{:S(2)}, u32[]{:S(2)}) %all-to-all-start.3) | async-done | bytes 442400 | tf_op jit(solution)/shard_map/all_to_all | solution.py:131
  275.9 5.2 all-to-all-start.2
  288.9 47.7 %all-to-all-done.2 = bf16[64,9,1152]{2,1,0:T(8,128)(2,1)S(1)} async-done(((bf16[64,9,1152]{2,1,0:T(8,128)(2,1)}), bf16[64,9,1152]{2,1,0:T(8,128)(2,1)S(1)}, u32[]{:S(2)}, u32[]{:S(2)}) %all-to-all-start.2) | async-done | bytes 1327136 | tf_op jit(solution)/shard_map/all_to_all | solution.py:137
  338.2 3.7 reshape.99
  342.0 3.3 convolution_convert_fusion.1
  345.3 63.0 %fusion.58 = (bf16[16,1152]{1,0:T(8,128)(2,1)S(1)}, bf16[16,384]{1,0:T(8,128)(2,1)S(1)}) fusion(bf16[384,1152]{1,0:T(8,128)(2,1)} %convolution_convert_fusion.1, bf16[384,384]{1,0:T(8,128)(2,1)} %convolution_convert_fusion.5), kind=kCustom, calls=%all-reduce-scatter.2 | all-reduce-scatter fusion | flops 786433 | bytes 1230848
  412.8 8.4 %collective-permute-start.13 = (bf16[16,384]{1,0:T(8,128)(2,1)S(1)}, bf16[16,384]{1,0:T(8,128)(2,1)S(1)}, u32[]{:S(2)}, u32[]{:S(2)}) collective-permute-start(bf16[16,384]{1,0:T(8,128)(2,1)S(1)} %get-tuple-element.29), channel_id=1, source_target_pairs={{0,4},{1,5},{2,6},{3,7},{4,8},{5,9},{6,10},{7,11},{8,12},{9,13},{1... | collective-permute-start | bytes 36872
  430.9 3.4 collective-permute-start.11
  434.3 2.8 collective-permute-start.10
  441.5 4.6 collective-permute-start.8
  447.7 4.5 collective-permute-start.6
  454.3 52.0 %all-reduce.4 = bf16[384]{0:T(512)(128)(2,1)S(1)} all-reduce(bf16[384]{0:T(512)(128)(2,1)S(1)} %get-tuple-element.20), channel_id=5, replica_groups=mesh['clip'=16,'tm'=32] {'tm'}, use_global_device_ids=true, to_apply=%region_12.13.clone | all-reduce | flops 384 | bytes 1536
  515.5 3.5 concatenate.12
  520.8 143.8 %all-reduce.11.cloned.1.call-done = bf16[3,384,384]{2,0,1:T(4,128)(2,1)} async-done(((bf16[3,384,384]{2,0,1:T(4,128)(2,1)}), bf16[3,384,384]{2,0,1:T(4,128)(2,1)}) %all-reduce.11.cloned.1.call-update) | async-done | bytes 884752
  665.4 63.6 %all-reduce.7 = (bf16[3,12,384]{2,0,1:T(4,128)(2,1)S(1)}, bf16[12,1152]{1,0:T(8,128)(2,1)S(1)}, bf16[12,384]{1,0:T(8,128)(2,1)S(1)}, bf16[12]{0:T(256)(128)(2,1)S(1)}) all-reduce(bf16[3,12,384]{2,0,1:T(4,128)(2,1)S(1)} %constant_dynamic-slice_fusion.2, ...), channel_id=1, replica_groups=mesh['clip'=16,'tm'=32] {'clip'}, use_global_device_ids=true, to_apply=%region_6.7 | all-reduce | flops 32268 | bytes 129072 | tf_op jit(solution)/shard_map/psum | solution.py:159
  (153 shorter events, 75.0 us)
Async XLA Ops:
  52.9 147.5 %all-to-all-start.1 = ((bf16[2,288,384]{2,0,1:T(2,128)(2,1)}), bf16[2,288,384]{2,0,1:T(2,128)(2,1)S(1)}, u32[]{:S(2)}, u32[]{:S(2)}) async-start(bf16[2,288,384]{2,0,1:T(2,128)(2,1)} %copy.36), calls=%async_computation.1 | async-start | bytes 884736 | tf_op jit(solution)/shard_map/all_to_all | solution.py:135
  56.6 137.5 %collective-permute-start = (bf16[2,288,384]{2,1,0:T(8,128)(2,1)S(1)}, bf16[2,288,384]{2,1,0:T(8,128)(2,1)}, u32[]{:S(2)}, u32[]{:S(2)}) collective-permute-start(bf16[2,288,384]{2,1,0:T(8,128)(2,1)S(1)} %bitcast.117), channel_id=1, source_target_pairs={{0,1},{1,2},{2,3},{3,4},{4,5},{5,6},{6,7},{7,8},{8,9},{9,10},{10,1... | collective-permute-start | bytes 1327112 | tf_op jit(solution)/shard_map/ppermute | solution.py:14
  200.4 43.0 %all-to-all-start = ((bf16[2,288,1152]{2,0,1:T(2,128)(2,1)}), bf16[2,288,1152]{2,0,1:T(2,128)(2,1)S(1)}, u32[]{:S(2)}, u32[]{:S(2)}) async-start(bf16[2,288,1152]{2,0,1:T(2,128)(2,1)} %copy.34), calls=%async_computation | async-start | bytes 2654208 | tf_op jit(solution)/shard_map/all_to_all | solution.py:126
  248.4 26.7 %all-to-all-start.3 = ((bf16[64,9,384]{2,1,0:T(8,128)(2,1)}), bf16[64,9,384]{2,1,0:T(8,128)(2,1)S(1)}, u32[]{:S(2)}, u32[]{:S(2)}) async-start(bf16[64,9,384]{2,1,0:T(8,128)(2,1)} %copy.46), calls=%async_computation.3 | async-start | bytes 1572864 | tf_op jit(solution)/shard_map/all_to_all | solution.py:131
  275.9 60.8 %all-to-all-start.2 = ((bf16[64,9,1152]{2,1,0:T(8,128)(2,1)}), bf16[64,9,1152]{2,1,0:T(8,128)(2,1)S(1)}, u32[]{:S(2)}, u32[]{:S(2)}) async-start(bf16[64,9,1152]{2,1,0:T(8,128)(2,1)} %copy.39), calls=%async_computation.2 | async-start | bytes 4718592 | tf_op jit(solution)/shard_map/all_to_all | solution.py:137
  281.2 383.4 %all-reduce.11.cloned.1.call-start = ((), (), s32[]{:S(2)}) async-start(), calls=%async_computation.4 | async-start | bytes 2359296
  408.3 22.6 %collective-permute-start.16 = (bf16[16,384]{1,0:T(8,128)(2,1)S(1)}, bf16[16,384]{1,0:T(8,128)(2,1)S(1)}, u32[]{:S(2)}, u32[]{:S(2)}) collective-permute-start(bf16[16,384]{1,0:T(8,128)(2,1)S(1)} %get-tuple-element.29), channel_id=1, source_target_pairs={{0,7},{1,8},{2,9},{3,10},{4,11},{5,12},{6,13},{7,14},{8,15},{9,16}... | collective-permute-start | bytes 36872
  409.6 24.7 %collective-permute-start.15 = (bf16[16,384]{1,0:T(8,128)(2,1)S(1)}, bf16[16,384]{1,0:T(8,128)(2,1)S(1)}, u32[]{:S(2)}, u32[]{:S(2)}) collective-permute-start(bf16[16,384]{1,0:T(8,128)(2,1)S(1)} %get-tuple-element.29), channel_id=1, source_target_pairs={{0,6},{1,7},{2,8},{3,9},{4,10},{5,11},{6,12},{7,13},{8,14},{9,15},... | collective-permute-start | bytes 36872
  410.9 28.5 %collective-permute-start.14 = (bf16[16,384]{1,0:T(8,128)(2,1)S(1)}, bf16[16,384]{1,0:T(8,128)(2,1)S(1)}, u32[]{:S(2)}, u32[]{:S(2)}) collective-permute-start(bf16[16,384]{1,0:T(8,128)(2,1)S(1)} %get-tuple-element.29), channel_id=1, source_target_pairs={{0,5},{1,6},{2,7},{3,8},{4,9},{5,10},{6,11},{7,12},{8,13},{9,14},{... | collective-permute-start | bytes 36872
  412.8 28.7 %collective-permute-start.13 = (bf16[16,384]{1,0:T(8,128)(2,1)S(1)}, bf16[16,384]{1,0:T(8,128)(2,1)S(1)}, u32[]{:S(2)}, u32[]{:S(2)}) collective-permute-start(bf16[16,384]{1,0:T(8,128)(2,1)S(1)} %get-tuple-element.29), channel_id=1, source_target_pairs={{0,4},{1,5},{2,6},{3,7},{4,8},{5,9},{6,10},{7,11},{8,12},{9,13},{1... | collective-permute-start | bytes 36872
  423.5 6.1 collective-permute-start.17
  429.6 16.4 %collective-permute-start.12 = (bf16[16,384]{1,0:T(8,128)(2,1)S(1)}, bf16[16,384]{1,0:T(8,128)(2,1)S(1)}, u32[]{:S(2)}, u32[]{:S(2)}) collective-permute-start(bf16[16,384]{1,0:T(8,128)(2,1)S(1)} %get-tuple-element.29), channel_id=1, source_target_pairs={{0,3},{1,4},{2,5},{3,6},{4,7},{5,8},{6,9},{7,10},{8,11},{9,12},{10... | collective-permute-start | bytes 36872
  430.9 16.7 %collective-permute-start.11 = (bf16[16,384]{1,0:T(8,128)(2,1)S(1)}, bf16[16,384]{1,0:T(8,128)(2,1)S(1)}, u32[]{:S(2)}, u32[]{:S(2)}) collective-permute-start(bf16[16,384]{1,0:T(8,128)(2,1)S(1)} %get-tuple-element.29), channel_id=1, source_target_pairs={{0,2},{1,3},{2,4},{3,5},{4,6},{5,7},{6,8},{7,9},{8,10},{9,11},{10,... | collective-permute-start | bytes 36872
  434.3 17.8 %collective-permute-start.10 = (bf16[16,384]{1,0:T(8,128)(2,1)S(1)}, bf16[16,384]{1,0:T(8,128)(2,1)S(1)}, u32[]{:S(2)}, u32[]{:S(2)}) collective-permute-start(bf16[16,384]{1,0:T(8,128)(2,1)S(1)} %get-tuple-element.29), channel_id=1, source_target_pairs={{0,1},{1,2},{2,3},{3,4},{4,5},{5,6},{6,7},{7,8},{8,9},{9,10},{10,1... | collective-permute-start | bytes 36872
  439.4 79.7 %copy-start.8 = (bf16[1,384,384]{2,0,1:T(2,128)(2,1)S(1)}, bf16[1,384,384]{2,0,1:T(2,128)(2,1)}, u32[]{:S(2)}) copy-start(bf16[1,384,384]{2,0,1:T(2,128)(2,1)} %get-tuple-element.30) | copy-start | bytes 884740
  439.4 79.7 %collective-permute-start.1 = (bf16[2,288,384]{2,1,0:T(8,128)(2,1)S(1)}, bf16[2,288,384]{2,1,0:T(8,128)(2,1)S(1)}, u32[]{:S(2)}, u32[]{:S(2)}) collective-permute-start(bf16[2,288,384]{2,1,0:T(8,128)(2,1)S(1)} %fusion.35), channel_id=1, source_target_pairs={{1,0},{2,1},{3,2},{4,3},{5,4},{6,5},{7,6},{8,7},{9,8},{10,9},{11,1... | collective-permute-start | bytes 1327112 | tf_op jit(solution)/shard_map/ppermute | solution.py:14
  441.5 67.5 %collective-permute-start.8 = (bf16[16,1152]{1,0:T(8,128)(2,1)S(1)}, bf16[16,1152]{1,0:T(8,128)(2,1)S(1)}, u32[]{:S(2)}, u32[]{:S(2)}) collective-permute-start(bf16[16,1152]{1,0:T(8,128)(2,1)S(1)} %get-tuple-element.28), channel_id=1, source_target_pairs={{0,7},{1,8},{2,9},{3,10},{4,11},{5,12},{6,13},{7,14},{8,15},{9,16}... | collective-permute-start | bytes 110600
  446.1 64.2 %collective-permute-start.7 = (bf16[16,1152]{1,0:T(8,128)(2,1)S(1)}, bf16[16,1152]{1,0:T(8,128)(2,1)S(1)}, u32[]{:S(2)}, u32[]{:S(2)}) collective-permute-start(bf16[16,1152]{1,0:T(8,128)(2,1)S(1)} %get-tuple-element.28), channel_id=1, source_target_pairs={{0,6},{1,7},{2,8},{3,9},{4,10},{5,11},{6,12},{7,13},{8,14},{9,15},... | collective-permute-start | bytes 110600
  447.7 63.9 %collective-permute-start.6 = (bf16[16,1152]{1,0:T(8,128)(2,1)S(1)}, bf16[16,1152]{1,0:T(8,128)(2,1)S(1)}, u32[]{:S(2)}, u32[]{:S(2)}) collective-permute-start(bf16[16,1152]{1,0:T(8,128)(2,1)S(1)} %get-tuple-element.28), channel_id=1, source_target_pairs={{0,5},{1,6},{2,7},{3,8},{4,9},{5,10},{6,11},{7,12},{8,13},{9,14},{... | collective-permute-start | bytes 110600
  452.2 55.5 %collective-permute-start.9 = (bf16[12,1152]{1,0:T(8,128)(2,1)S(1)}, bf16[12,1152]{1,0:T(8,128)(2,1)S(1)}, u32[]{:S(2)}, u32[]{:S(2)}) collective-permute-start(bf16[12,1152]{1,0:T(8,128)(2,1)S(1)} %slice.41), channel_id=1, source_target_pairs={{0,8},{1,9},{2,10},{3,11},{4,12},{5,13},{6,14},{7,15},{8,16},{9,17... | collective-permute-start | bytes 82952
  507.7 5.9 collective-permute-start.5
  509.0 4.6 collective-permute-start.4
  510.3 3.3 collective-permute-start.3
  511.6 3.9 collective-permute-start.2
  (29 other events, 452.9 us)
Sparse Core Ops, SparseCore 0:
  439.5 225.0 all-reduce.10
where the time goes:
time: 752 us; the launch traced here: 738 us
  blocking collectives  350 us (47%)
  waiting for transfers between devices  237 us (32%)
  starting transfers between devices  68.6 us (9%)
  local copies, waits for them, and re-layouts  34.5 us (5%)
  matrix products  27.1 us (4%)
  between operations  16.9 us (2%)
    unnamed x3, blocking collectives  168 us
    unnamed x18, waiting for transfers between devices  145 us
    psum x1, blocking collectives, body(): lax.psum(shards[0].astype(jnp.bfloat16), 'clip').astype(jnp.float32)  63.6 us
    all_to_all x1, waiting for transfers between devices, body(): lax.all_to_all(grad_packed, 'tm', split_axis=0, concat_axis=1, tiled=True)  47.7 us
    all_gather x1, blocking collectives, body(): lax.all_gather(out_w, 'tm', axis=0, tiled=True)  43 us
    all_gather x1, blocking collectives, body(): lax.all_gather(conv_w, 'tm', axis=1, tiled=True)  41.5 us
    unnamed x17, starting transfers between devices  40.7 us
    all_gather x1, blocking collectives, body(): lax.all_gather(qkv_w, 'tm', axis=0, tiled=True)  33.9 us
  transfers between devices with their start and end apart: 23, of which 5 were waited for; matrix products, arithmetic and copies ran while one was open for 6% of the time, Pallas kernels for 0%

commit v1 on v0

v1 whole, which is shorter than its diff:
```python
import functools
import math

import jax
import jax.numpy as jnp
from jax import lax
from jax.experimental import pallas as pl
from jax.experimental.pallas import tpu as pltpu
from jax.sharding import PartitionSpec as P

epsilon = 1e-06
F32 = jnp.float32
BF16 = jnp.bfloat16

C = 384
FRAMES = 64
SPOTS = 9
ROWS = SPOTS * FRAMES
PARTS = ((0, 5), (5, 4))
BLOCKS = (((0, 192), (192, 128)), ((0, 128), (128, 128)))
MATS = 7
WIDE = MATS * C


def mm(a, b):
    return lax.dot_general(a, b, (((1,), (0,)), ((), ())), preferred_element_type=F32)


def mm_nt(a, b):
    return lax.dot_general(a, b, (((1,), (1,)), ((), ())), preferred_element_type=F32)


def mm_tn(a, b):
    return lax.dot_general(a, b, (((0,), (0,)), ((), ())), preferred_element_type=F32)


def iotas(rows, columns):
    shape = (rows, columns)
    return lax.broadcasted_iota(jnp.int32, shape, 0), lax.broadcasted_iota(jnp.int32, shape, 1)


def delay_matrix(size, steps):
    row, col = iotas(size, size)
    return jnp.where((row - col == steps) & ((row & (FRAMES - 1)) >= steps), 1.0, 0.0).astype(BF16)


def forward(blocks, w, gain, x, s1, s2, hidden, inverse, normed, packed):
    for steps, ref in ((1, s1), (2, s2)):
        for first, size in blocks:
            rows = pl.ds(first, size)
            ref[rows, :] = mm(delay_matrix(size, steps), x[rows, :]).astype(BF16)
    mixed = mm(x[...], w[:, 0:C]) + mm(s1[...], w[:, C : 2 * C]) + mm(s2[...], w[:, 2 * C : 3 * C])
    hidden[...] = (x[...].astype(F32) + mixed).astype(BF16)
    wide = hidden[...].astype(F32)
    inverse[...] = lax.rsqrt(jnp.mean(wide * wide, axis=-1, keepdims=True) + epsilon)
    normed[...] = (wide * inverse[...] * gain[...]).astype(BF16)
    packed[...] = mm(normed[...], w[:, 3 * C : 6 * C]).astype(BF16)


def seen(size):
    row, col = iotas(size, size)
    return ((row >> 6) == (col >> 6)) & (col <= row)


def attention(blocks, w, cot, packed, attended, grad_att, grad_packed):
    factor = 1.0 / math.sqrt(C)
    grad_att[...] = mm_nt(cot[...], w[:, 6 * C : 7 * C]).astype(BF16)
    for first, size in blocks:
        part = pl.ds(first, size)
        query, keys, values = (packed[part, i * C : (i + 1) * C] for i in range(3))
        scores = jnp.where(seen(size), mm_nt(query, keys) * factor, -1e30)
        raised = jnp.exp(scores - jnp.max(scores, axis=-1, keepdims=True))
        probs = raised / jnp.sum(raised, axis=-1, keepdims=True)
        rounded = probs.astype(BF16)
        attended[part, :] = mm(rounded, values).astype(BF16)
        incoming = grad_att[part, :]
        dprob = mm_nt(incoming, values)
        dscore = probs * (dprob - jnp.sum(dprob * probs, axis=-1, keepdims=True))
        dscore = (dscore * factor).astype(BF16)
        grad_packed[part, 0:C] = mm(dscore, keys).astype(BF16)
        grad_packed[part, C : 2 * C] = mm_tn(dscore, query).astype(BF16)
        grad_packed[part, 2 * C : 3 * C] = mm_tn(rounded, incoming).astype(BF16)


def normalize_back(w, gain, cot, hidden, inverse, grad_packed, grad_hidden):
    grad_norm = mm_nt(grad_packed[...], w[:, 3 * C : 6 * C]).astype(BF16).astype(F32)
    wide = hidden[...].astype(F32)
    inv = inverse[...]
    scaled = grad_norm * gain[...]
    inner = jnp.mean(scaled * wide, axis=-1, keepdims=True)
    back = cot[...].astype(F32) + inv * scaled - wide * (inv * inv * inv * inner)
    grad_hidden[...] = back.astype(BF16)
    return jnp.sum(grad_norm * wide * inv, axis=0, keepdims=True)


def conv_back(blocks, w, grad_hidden, a1, a2, gv):
    for steps, ref in ((1, a1), (2, a2)):
        for first, size in blocks:
            rows = pl.ds(first, size)
            ref[rows, :] = mm_tn(delay_matrix(size, steps), grad_hidden[rows, :]).astype(BF16)
    grad = grad_hidden[...].astype(F32) + mm_nt(grad_hidden[...], w[:, 0:C])
    grad = grad + mm_nt(a1[...], w[:, C : 2 * C]) + mm_nt(a2[...], w[:, 2 * C : 3 * C])
    gv[...] = grad.astype(BF16)


WAYS = 32
PIECE = 112
CUTS = ((0, 64), (64, 48))
BACK = 64
SHARE = 12
QUAD = 4 * SHARE
HALF = C // 2
MESH = pl.DeviceIdType.MESH
FAR_FIRST = (4, 3, 5, 2, 6, 1, 7)


def ninth(n):
    return (n * 57) >> 9


def fifth(n):
    return (n * 205) >> 10


def twelfth(n):
    return (n * 1366) >> 14


def picks(target, rows, columns):
    row, col = iotas(rows, columns)
    return jnp.where(col == target(row), 1.0, 0.0).astype(BF16)


class Place:
    def __init__(self):
        self.clip, self.tm = lax.axis_index("clip"), lax.axis_index("tm")
        self.y, self.z = lax.rem(self.clip, 8), lax.div(self.tm, 4)
        self.low = lax.rem(lax.div(self.tm, 2), 2)
        self.x = lax.div(self.clip, 8) * 2 + self.low
        self.core = lax.rem(self.tm, 2)
        self.rail = self.low * 2 + self.core

    def at(self, dx=0, dy=0, dz=0, other=False):
        x, y, z = lax.rem(self.x + dx, 4), lax.rem(self.y + dy, 8), lax.rem(self.z + dz, 8)
        core = 1 - self.core if other else self.core
        return (lax.div(x, 2) * 8 + y, z * 4 + lax.rem(x, 2) * 2 + core)

    def peer(self, k):
        return (self.clip, lax.rem(self.tm + k, WAYS))


def greet(me, outer):
    barrier = pltpu.get_barrier_semaphore()

    def tell(device):
        pl.semaphore_signal(barrier, inc=1, device_id=device, device_id_type=MESH)

    def step(k, carry):
        tell(me.peer(k))
        return carry

    lax.fori_loop(1, WAYS, step, 0)
    for k in range(1, 8):
        tell(me.at(dy=k))
    for device in outer:
        tell(device)
    return lambda: pl.semaphore_wait(barrier, WAYS - 1 + 7 + len(outer))


def remote(src, dst, sems, index, device):
    return pltpu.make_async_remote_copy(
        src_ref=src, dst_ref=dst, send_sem=sems[0].at[index], recv_sem=sems[1].at[index],
        device_id=device, device_id_type=MESH,
    )


def settle(ref, sem):
    pltpu.make_async_copy(ref, ref, sem).wait()


def each_peer(act, first=0, last=WAYS - 1):
    def step(i, carry):
        act(lax.rem(i + 12, WAYS - 1) + 1)
        return carry

    lax.fori_loop(first, last, step, 0)


class Exchange:
    def __init__(self, me, src, dst, cuts, sems, hops, hop_sems):
        self.__dict__.update(locals())

    def send(self, part, k):
        me, rows = self.me, pl.ds(*self.cuts[part])
        device = me.peer(k)
        target = device[1]
        opposite = lax.rem(me.z + 4, 8) == lax.div(target, 4)
        over = opposite & (lax.rem(target, 2) != me.core)
        piece = self.src.at[target, rows]

        @pl.when(over)
        def _():
            slot = self.hops.at[part, lax.rem(lax.div(target, 2), 2), pl.ds(0, self.cuts[part][1])]
            pltpu.make_async_remote_copy(
                src_ref=piece, dst_ref=slot, send_sem=self.sems[0].at[part],
                recv_sem=self.hop_sems[1].at[part], device_id=me.at(dz=6), device_id_type=MESH,
            ).start()

        @pl.when(jnp.logical_not(over))
        def _():
            remote(piece, self.dst.at[me.tm, rows], self.sems, part, device).start()

    def forward(self, part):
        me, size = self.me, self.cuts[part][1]
        self.settle_hops(part, self.hop_sems[1])
        source, target = me.at(dz=2)[1], me.at(dz=6, other=True)
        for low in range(2):
            device = (target[0], lax.div(target[1], 4) * 4 + low * 2 + 1 - me.core)
            pltpu.make_async_remote_copy(
                src_ref=self.hops.at[part, low, pl.ds(0, size)],
                dst_ref=self.dst.at[source, pl.ds(*self.cuts[part])],
                send_sem=self.hop_sems[0].at[part], recv_sem=self.sems[1].at[part],
                device_id=device, device_id_type=MESH,
            ).start()

    def settle_hops(self, part, sems):
        settle(self.hops.at[part, :, pl.ds(0, self.cuts[part][1])], sems.at[part])

    def arrive(self, part):
        settle(self.dst.at[pl.ds(0, WAYS - 1), pl.ds(*self.cuts[part])], self.sems[1].at[part])

    def drain(self):
        for part in range(2):
            settle(self.src.at[pl.ds(0, WAYS - 1), pl.ds(*self.cuts[part])], self.sems[0].at[part])
            self.settle_hops(part, self.hop_sems[0])


def pack_in(d, video, cot, out):
    base = lax.min(lax.div(d * SPOTS, 16) * 16, 256)
    base = pl.multiple_of(base, 16)
    pieces = [
        ref[0, f, pl.ds(base, 32), c * 128 : (c + 1) * 128]
        for ref in (video, cot) for c in range(3) for f in range(2)
    ]
    shift = d * SPOTS - base

    def column(r):
        block = jnp.where(r < 64, fifth(r), (r - 64) >> 2)
        spot = jnp.where(r < 64, r - fifth(r) * 5, 5 + (r & 3))
        return block * 32 + spot + shift

    pick = picks(column, PIECE, 384)
    out[d] = mm(pick, jnp.concatenate(pieces, 0)).astype(BF16)


def pack_weights(tm, conv, qkv, out_w, gain, shard):
    row, col = iotas(SHARE, C)
    own = col == tm * SHARE + row
    line = mm(gain[...], jnp.where(own, 1.0, 0.0).astype(BF16))
    diagonal = jnp.where(own, line, 0.0).astype(BF16)
    mats = [conv[0], conv[1], conv[2], qkv[:, 0:C], qkv[:, C : 2 * C], qkv[:, 2 * C : 3 * C], out_w[...], diagonal]
    for h in range(2):
        total = 0.0
        for j in range(4):
            total = total + mm(picks(lambda r: r - j * SHARE, QUAD, SHARE), mats[4 * h + j])
        shard[h] = total.astype(BF16)


def unpack_in(part, landed, x, cot):
    (start, rows), spots = CUTS[part], PARTS[part][1]
    for a, ref in ((0, x), (1, cot)):
        for c in range(3):
            first = (a * 3 + c) * 2 * spots
            base = min(first // 16 * 16, rows - 32)

            def column(r):
                return ((r & 15) >> 1) * 32 + (r & 1) * spots + (r >> 4) + (first - base)

            pick = picks(column, spots * 16, 256)
            for g in range(4):
                source = landed[8 * g : 8 * g + 8, start + base : start + base + 32, :]
                got = mm(pick, source.reshape(256, 128)).astype(BF16)
                for p in range(spots):
                    row = p * FRAMES + 16 * g
                    ref[row : row + 16, c * 128 : (c + 1) * 128] = got[16 * p : 16 * p + 16]


def unpack_weights(weights, w, gain):
    for m in range(MATS + 1):
        h, j = m // 4, m % 4
        base, size = ((0, 16), (0, 32), (16, 32), (32, 16))[j]

        def column(r):
            block = twelfth(r)
            return ((block & 3) * 8 + (block >> 2)) * size + (r - block * SHARE) + j * SHARE - base

        source = weights[h, :, :, base : base + size, :].reshape(WAYS * size, C)
        got = mm(picks(column, C, WAYS * size), source)
        if m < MATS:
            w[:, m * C : (m + 1) * C] = got.astype(BF16)
        else:
            gain[...] = jnp.sum(got, axis=0, keepdims=True)


def pack_out(part, gv, out):
    spots = PARTS[part][1]

    def column(r):
        inner = r & 31
        block = fifth(inner) if spots == 5 else inner >> 2
        spot = inner - block * spots
        return (block >> 1) * (16 * spots) + spot * 16 + (r >> 5) * 2 + (block & 1)

    pick = picks(column, 256, 48 * spots)
    for g in range(4):
        pieces = [
            gv[p * FRAMES + 16 * g : p * FRAMES + 16 * g + 16, c * 128 : (c + 1) * 128]
            for c in range(3) for p in range(spots)
        ]
        got = mm(pick, jnp.concatenate(pieces, 0)).astype(BF16)
        out[8 * g : 8 * g + 8, 32 * part : 32 * part + 32, :] = got.reshape(8, 32, 128)


def unpack_out(landed, grad_video):
    for f in range(2):
        for c in range(3):

            def column(r):
                spot = r - ninth(r) * SPOTS
                inner = jnp.where(spot < 5, c * 10 + f * 5 + spot, 32 + c * 8 + f * 4 + spot - 5)
                return ninth(r) * BACK + inner

            pick = picks(column, 144, 16 * BACK)
            for h in range(2):
                source = landed[16 * h : 16 * h + 16].reshape(16 * BACK, 128)
                got = mm(pick, source).astype(BF16)
                grad_video[0, f, 144 * h : 144 * h + 144, c * 128 : (c + 1) * 128] = got


def gather_weights(me, shard, weights, z_sems, y_sems, x_sems, c_sems):
    half = lax.rem(me.y, 2)
    begun = []

    def go(copy):
        copy.start()
        begun.append(copy)
        return copy

    def block(dz, *rows):
        return weights.at[half, me.rail, lax.rem(me.z + dz, 8), *rows]

    def over_z():
        for k in (2, 6, 1, 7):
            go(remote(shard.at[half], block(0), z_sems, k, me.at(dz=k)))
        weights[half, me.rail, me.z] = shard[half]

    def onward():
        for copy in begun[:2]:
            copy.wait_recv()
        top, low = pl.ds(0, 32), pl.ds(32, 16)
        go(remote(block(6, top), block(6, top), z_sems, 4, me.at(dz=2)))
        go(remote(block(2, low), block(2, low), z_sems, 0, me.at(dz=6)))
        go(remote(block(6), block(6), z_sems, 3, me.at(dz=1)))
        go(remote(block(2), block(2), z_sems, 5, me.at(dz=7)))

    def rest(between):
        for copy in begun[2:]:
            copy.wait_recv()
        beyond = (1 - me.low) * 2 + me.core
        part = lambda h, rail, i: weights.at[h, rail, pl.ds(4 * i, 4)]
        ys, xs, cs = [], [], []
        for i, step in ((0, 1), (1, 7)):
            mine = part(half, me.rail, i)
            ys.append(go(remote(mine, mine, y_sems, i, me.at(dy=step))))
        for i, step in ((0, 1), (1, 3)):
            mine = part(half, me.rail, i)
            xs.append(go(remote(mine, mine, x_sems, i, me.at(dx=step))))
            cs.append(go(remote(mine, mine, c_sems, i, me.at(other=True))))
        between()
        for i, step in ((0, 1), (1, 3)):
            ys[i].wait_recv()
            mine = part(1 - half, me.rail, i)
            xs.append(go(remote(mine, mine, x_sems, 2 + i, me.at(dx=step))))
            cs.append(go(remote(mine, mine, c_sems, 2 + i, me.at(other=True))))
        for n in range(4):
            xs[n].wait_recv()
            mine = part(half if n < 2 else 1 - half, beyond, n % 2)
            cs.append(go(remote(mine, mine, c_sems, 4 + n, me.at(other=True))))
        for copy in cs:
            copy.wait_recv()

    def drain():
        for copy in begun:
            copy.wait_send()

    return over_z, onward, rest, drain


class Sums:
    def __init__(self, me, sums, core_in, held, mid, x_in, z_in, y_in, y_out, totals, sems):
        self.__dict__.update(locals())
        self.round = lax.rem(me.x + me.core, 2)
        self.mine = lax.div(me.x, 2)

    def to_core(self, r, i):
        slot = lax.rem(self.me.core + 1 + r, 2) + 2 * i
        return remote(
            self.sums.at[r, slot], self.core_in.at[r, i], self.sems["c"], 2 * r + i,
            self.me.at(other=True),
        )

    def to_mid(self, r, i):
        part = self.held.at[r, 1 - self.mine, pl.ds(i * HALF, HALF)]
        return remote(part, self.mid.at[i], self.sems["m"], 2 * r + i, self.me.at(dx=3 if i else 1))

    def to_owner(self, r, i):
        step = 3 if i else 1
        which = lax.div(lax.rem(self.me.x + step, 4), 2)
        copy = remote(
            self.held.at[r, which], self.x_in.at[i], self.sems["x"], 2 * r + i, self.me.at(dx=step)
        )
        return which, copy

    def over_z(self, k):
        first = pl.multiple_of(lax.rem(self.me.z + k, 8) * QUAD, QUAD)
        part = self.held.at[self.round, self.mine, pl.ds(first, QUAD)]
        return remote(part, self.z_in.at[k], self.sems["z"], 0, self.me.at(dz=k))

    def over_y(self, k):
        mine = self.y_in.at[self.me.y]
        return remote(mine, mine, self.sems["y"], 0, self.me.at(dy=k))

    def over_row(self, k):
        dx, other = ((2, False), (2, True), (1, False), (3, False), (1, True), (3, True), (0, True))[k]
        own = self.round * 4 + self.me.x
        return remote(
            self.y_out, self.totals.at[own], self.sems["f"], 0, self.me.at(dx=dx, other=other)
        )

    def when_owner(self, r, act):
        pl.when(self.round == r)(act)

    def core_send(self, r):
        for i in range(2):
            self.to_core(r, i).start()

    def core_add(self, r):
        for i in range(2):
            self.to_core(r, i).wait_recv()
            slot = lax.rem(self.me.core + r, 2) + 2 * i
            both = self.sums[r, slot].astype(F32) + self.core_in[r, i].astype(F32)
            self.held[r, i] = both.astype(BF16)

        def act():
            for i in range(2):
                self.to_mid(r, i).start()

        self.when_owner(r, act)

    def relay(self, r):
        def act():
            for i in range(2):
                self.to_mid(r, i).wait_recv()
                which, copy = self.to_owner(r, i)
                rows = pl.ds(i * HALF, HALF)
                both = self.held[r, which, rows, :].astype(F32) + self.mid[i].astype(F32)
                self.held[r, which, rows, :] = both.astype(BF16)
                copy.start()

        self.when_owner(1 - r, act)

    def own_x(self, r):
        def act():
            total = self.held[r, self.mine].astype(F32)
            for i in range(2):
                self.to_owner(r, i)[1].wait_recv()
                total = total + self.x_in[i].astype(F32)
            self.held[r, self.mine] = total.astype(BF16)
            for k in FAR_FIRST:
                self.over_z(k).start()

        self.when_owner(r, act)

    def own_z(self):
        here = pl.ds(pl.multiple_of(self.me.z * QUAD, QUAD), QUAD)
        total = self.held[self.round, self.mine, here, :].astype(F32)
        settle(self.z_in.at[pl.ds(1, 7)], self.sems["z"][1].at[0])
        for k in range(1, 8):
            total = total + self.z_in[k].astype(F32)
        self.y_in[self.me.y] = total.astype(BF16)
        for k in FAR_FIRST:
            self.over_y(k).start()

    def own_y(self):
        settle(self.y_in.at[pl.ds(1, 7)], self.sems["y"][1].at[0])
        total = self.y_in[0].astype(F32)
        for k in range(1, 8):
            total = total + self.y_in[k].astype(F32)
        self.y_out[...] = total.astype(BF16)
        for k in range(7):
            self.over_row(k).start()
        self.totals[self.round * 4 + self.me.x] = self.y_out[...]

    def drain(self):
        for sem in (*self.sems["f"], self.sems["z"][0], self.sems["y"][0]):
            settle(self.z_in.at[pl.ds(1, 7)], sem.at[0])
        for r in range(2):
            for i in range(2):
                self.to_core(r, i).wait_send()

            def owner(r=r):
                for i in range(2):
                    self.to_mid(r, i).wait_send()

            def other(r=r):
                for i in range(2):
                    self.to_owner(r, i)[1].wait_send()

            self.when_owner(r, owner)
            self.when_owner(1 - r, other)


def main_kernel(
    video_in, cot_in, conv_in, qkv_in, out_in, gain_in, grad_video, totals,
    video, cotangent, conv, qkv, out_w, parcels, shard, landed, weights,
    w, gain, parcels_out, landed_out, hops_in, hops_out, acc, gain_acc,
    x, cot, s1, s2, hidden, inverse, normed, packed, attended, grad_att, grad_packed,
    grad_hidden, a1, a2, gv,
    sums, core_in, held, mid, x_in, z_in, y_in, y_out,
    l_s, i_s, i_r, o_s, o_r, h_s, h_r, g_s, g_r, wz_s, wz_r, wy_s, wy_r, wx_s, wx_r, wc_s, wc_r,
    sc_s, sc_r, sm_s, sm_r, sx_s, sx_r, sz_s, sz_r, sy_s, sy_r, sf_s, sf_r,
):
    me = Place()
    pairs = (
        (conv_in, conv), (qkv_in, qkv), (out_in, out_w), (video_in, video), (cot_in, cotangent)
    )
    reads = [pltpu.make_async_copy(src, dst, l_s.at[n]) for n, (src, dst) in enumerate(pairs)]
    for copy in reads:
        copy.start()
    outer = jnp.where(me.low == 0, 3, 1)
    met = greet(me, [me.at(dx=dx, other=o) for dx in (2, outer) for o in (False, True)])
    for copy in reads[:3]:
        copy.wait()
    pack_weights(me.tm, conv, qkv, out_w, gain_in, shard)
    for copy in reads[3:]:
        copy.wait()
    met()

    over_z, onward, rest, drain = gather_weights(
        me, shard, weights, (wz_s, wz_r), (wy_s, wy_r), (wx_s, wx_r), (wc_s, wc_r)
    )
    over_z()

    coming = Exchange(me, parcels, landed, CUTS, (i_s, i_r), hops_in, (h_s, h_r))
    going = Exchange(
        me, parcels_out, landed_out, ((0, 32), (32, 32)), (o_s, o_r), hops_out, (g_s, g_r)
    )

    def pack_and_send(k):
        pack_in(me.peer(k)[1], video, cotangent, parcels)
        coming.send(0, k)

    each_peer(pack_and_send, 0, 10)
    onward()
    each_peer(pack_and_send, 10)
    coming.forward(0)
    pack_in(me.tm, video, cotangent, landed)
    rest(lambda: each_peer(lambda k: coming.send(1, k)))
    coming.forward(1)
    unpack_weights(weights, w, gain)

    total = Sums(
        me, sums, core_in, held, mid, x_in, z_in, y_in, y_out, totals,
        dict(
            c=(sc_s, sc_r), m=(sm_s, sm_r), x=(sx_s, sx_r), z=(sz_s, sz_r), y=(sy_s, sy_r),
            f=(sf_s, sf_r),
        ),
    )
    tall = (
        x, cot, s1, s2, hidden, inverse, normed, packed, attended, grad_att, grad_packed,
        grad_hidden, a1, a2, gv,
    )
    for part, (first, spots) in enumerate(PARTS):
        rows = pl.ds(first * FRAMES, spots * FRAMES)
        (
            px, pcot, ps1, ps2, phidden, pinverse, pnormed, ppacked, pattended, pgrad_att,
            pgrad_packed, pgrad_hidden, pa1, pa2, pgv,
        ) = (ref.at[rows] for ref in tall)
        blocks = BLOCKS[part]
        coming.arrive(part)
        unpack_in(part, landed, px, pcot)
        if part == 1:
            going.forward(0)
        forward(blocks, w, gain, px, ps1, ps2, phidden, pinverse, pnormed, ppacked)
        attention(blocks, w, pcot, ppacked, pattended, pgrad_att, pgrad_packed)

        def add(n, left, right):
            product = mm_tn(left, right)
            if part == 0:
                acc[n] = product
            else:
                sums[n // 4, n % 4] = (acc[n] + product).astype(BF16)

        def early_sums():
            add(0, pattended[...], pcot[...])
            for i in range(3):
                add(1 + i, pnormed[...], pgrad_packed[:, i * C : (i + 1) * C])

        def late_sums():
            for tap, ref in enumerate((px, ps1, ps2)):
                add(4 + tap, ref[...], pgrad_hidden[...])

        def send_back():
            pack_out(part, pgv, parcels_out)
            landed_out[me.tm, 32 * part : 32 * part + 32, :] = (
                parcels_out[me.tm, 32 * part : 32 * part + 32, :]
            )

        def norm_back():
            return normalize_back(w, gain, pcot, phidden, pinverse, pgrad_packed, pgrad_hidden)

        if part == 0:
            gain_acc[...] = norm_back()
            conv_back(blocks, w, pgrad_hidden, pa1, pa2, pgv)
            send_back()
            each_peer(lambda k: going.send(0, k))
            early_sums()
            late_sums()
        else:
            early_sums()
            total.core_send(0)
            gain_sum = gain_acc[...] + norm_back()
            row, col = iotas(C, C)
            sums[1, 3] = jnp.where(row == col, gain_sum, 0.0).astype(BF16)
            late_sums()
            total.core_send(1)
            total.core_add(0)
            conv_back(blocks, w, pgrad_hidden, pa1, pa2, pgv)
            total.relay(0)
            total.core_add(1)
            send_back()
            total.own_x(0)
            each_peer(lambda k: going.send(1, k))
    total.relay(1)
    total.own_x(1)
    going.forward(1)
    total.own_z()
    for part in range(2):
        going.arrive(part)
    unpack_out(landed_out, grad_video)
    total.own_y()
    total.drain()
    drain()
    coming.drain()
    going.drain()


def call(kernel, outs, scratch, places, out_places, collective=None):
    extra = {} if collective is None else dict(collective_id=collective, has_side_effects=True)
    return pl.pallas_call(
        kernel,
        out_shape=[jax.ShapeDtypeStruct(*o) for o in outs],
        in_specs=[pl.BlockSpec(memory_space=place) for place in places],
        out_specs=[pl.BlockSpec(memory_space=place) for place in out_places],
        scratch_shapes=scratch,
        compiler_params=pltpu.CompilerParams(vmem_limit_bytes=56 * 1024 * 1024, **extra),
    )


def main(*args):
    def held(*shape, kind=BF16):
        return pltpu.VMEM(shape, kind)

    tall = held(ROWS, C)
    scratch = [
        held(1, 2, 288, C), held(1, 2, 288, C), held(3, SHARE, C), held(SHARE, 3 * C), held(SHARE, C),
        held(WAYS, PIECE, 128), held(2, QUAD, C), held(WAYS, PIECE, 128), held(2, 4, 8, QUAD, C),
        held(C, WIDE), held(1, C, kind=F32), held(WAYS, BACK, 128), held(WAYS, BACK, 128),
        held(2, 2, 64, 128), held(2, 2, 32, 128), held(MATS, C, C, kind=F32),
        held(1, C, kind=F32),
        tall, tall, tall, tall, tall, held(ROWS, 1, kind=F32), tall, held(ROWS, 3 * C), tall, tall,
        held(ROWS, 3 * C), tall, tall, tall, tall,
        held(2, 4, C, C), held(2, 2, C, C), held(2, 2, C, C), held(2, HALF, C), held(2, C, C),
        held(8, QUAD, C), held(8, QUAD, C), held(QUAD, C),
    ]
    counts = [5] + [2] * 8 + [8, 8, 2, 2, 4, 4, 8, 8] + [4] * 6 + [1] * 6
    scratch += [pltpu.SemaphoreType.DMA((n,)) for n in counts]
    outs = [(args[0].shape, BF16), ((8, QUAD, C), BF16)]
    places = [pl.ANY] * 5 + [pltpu.VMEM]
    return call(main_kernel, outs, scratch, places, [pltpu.VMEM] * 2, 1)(*args)


def finish_kernel(factor, grad_in, totals, grad_video, conv, qkv, out_w, gain, sem):
    copy = pltpu.make_async_copy(grad_in, grad_video, sem)
    copy.start()
    tm = lax.axis_index("tm")
    pick = picks(lambda r: r + lax.rem(tm, 4) * SHARE, 16, QUAD)
    got = [mm(pick, totals[m]) for m in range(8)]
    for i in range(3):
        conv[i] = got[4 + i][0:SHARE] * factor
        qkv[:, i * C : (i + 1) * C] = got[1 + i][0:SHARE] * factor
    out_w[...] = got[0][0:SHARE] * factor
    row, col = iotas(C, SHARE)
    line = mm(got[7].astype(BF16), jnp.where(row == tm * SHARE + col, 1.0, 0.0).astype(BF16))
    row, col = iotas(16, SHARE)
    gain[...] = jnp.sum(jnp.where(row == col, line, 0.0), axis=0, keepdims=True) * factor
    copy.wait()


def body(video, conv_w, qkv_w, out_w, gain, cotangent):
    grad_video, totals = main(video, cotangent, conv_w, qkv_w, out_w, gain.reshape(1, SHARE))
    factor = 1.0 / math.sqrt(
        lax.axis_size("clip") * lax.axis_size("tm") * video.shape[1] * video.shape[2]
    )
    outs = [
        (video.shape, BF16), (conv_w.shape, F32), (qkv_w.shape, F32), (out_w.shape, F32),
        ((1, SHARE), F32),
    ]
    got = call(
        functools.partial(finish_kernel, factor), outs, [pltpu.SemaphoreType.DMA],
        [pltpu.VMEM] * 2, [pl.ANY] + [pltpu.VMEM] * 4,
    )(grad_video, totals)
    return (*got[:4], got[4].reshape(SHARE))


def solution(mesh):
    in_specs = (
        P("clip", "tm", None, None),
        P(None, "tm", None),
        P("tm", None),
        P("tm", None),
        P("tm"),
        P("clip", "tm", None, None),
    )
    out_specs = (
        P("clip", "tm", None, None),
        P(None, "tm", None),
        P("tm", None),
        P("tm", None),
        P("tm"),
    )
    return jax.shard_map(body, mesh=mesh, in_specs=in_specs, out_specs=out_specs, check_vma=False)
```

time: 752 us -> 106 us (0.14); the launches traced: 738 us -> 106 us
  blocking collectives: 350 us -> 0 us
  waiting for transfers between devices: 237 us -> 0 us
  Pallas kernels: 0 us -> 105 us
  starting transfers between devices: 68.6 us -> 0 us
  local copies, waits for them, and re-layouts: 34.5 us -> 0 us
  matrix products: 27.1 us -> 0 us
  between operations: 16.9 us -> 0.8 us
    unnamed x3 -> x0, blocking collectives: 168 us -> none
    unnamed x18 -> x0, waiting for transfers between devices: 145 us -> none
    all_gather x3 -> x0, blocking collectives: 118 us -> none  [the longest x1 43 us: body(): lax.all_gather(out_w, 'tm', axis=0, tiled=True)]
    pallas_call x0 -> x2, Pallas kernels: none -> 105 us  [the longest x1 103 us: main(): return call(main_kernel, outs, scratch, places, [pltpu.VMEM] * 2, 1)(*args)]
    all_to_all x4 -> x0, waiting for transfers between devices: 92.9 us -> none  [the longest x1 47.7 us: body(): lax.all_to_all(grad_packed, 'tm', split_axis=0, concat_axis=1, tiled=True)]
    psum x1 -> x0, blocking collectives: 63.6 us -> none  [body(): lax.psum(shards[0].astype(jnp.bfloat16), 'clip').astype(jnp.float32)]
    unnamed x17 -> x0, starting transfers between devices: 40.7 us -> none
    dot_general x20 -> x0, matrix products: 27.1 us -> none  [the longest x9 10.4 us: project(): product = jnp.dot(flat, matrix, preferred_element_type=jnp.float32)]
  transfers between devices with their start and end apart: 23 -> 0, of which waited for: 5 -> 0; matrix products, arithmetic and copies ran while one was open for 6% -> 0% of each run, Pallas kernels for 0% -> 0%
where the time goes in v1:
time: 106 us
  Pallas kernels  105 us (99%)
    pallas_call x1, Pallas kernels, main(): return call(main_kernel, outs, scratch, places, [pltpu.VMEM] * 2, 1)(*args)  103 us
    pallas_call x1, Pallas kernels, body(): call(functools.partial(finish_kernel, factor), outs, [pltpu.SemaphoreType...  2.53 us

profile of v1, /device:TPU:1, one launch (start us, length us, event | category | flops | bytes accessed | tf_op | source)
XLA Modules:
  0.0 106.3 jit_solution(4567924303994943526)
XLA Ops:
  0.6 103.0 %shard_map.101 = (bf16[1,2,288,384]{3,2,1,0:T(8,128)(2,1)}, bf16[8,48,384]{2,1,0:T(8,128)(2,1)}) custom-call(bf16[1,2,288,384]{3,2,1,0:T(8,128)(2,1)} %video_in.1, bf16[1,2,288,384]{3,2,1,0:T(8,128)(2,1)} %cot_in.1, bf16[3,12,384]{2,1,0:T(8,128)(2,1)} %conv_in.1, bf16[12,1152]{1,0:T(8,128)(2,1)} %qkv_in.1, bf16[12,384]{1,0:T(8,128)(2,1)} %out_in.1, ...), custom_call_target="tpu_custom_call" | custom-call | tf_op jit(solution)/shard_map/pallas_call | solution.py:690
  103.6 2.5 %shard_map.102 = (bf16[1,2,288,384]{3,2,1,0:T(8,128)(2,1)}, f32[3,12,384]{2,1,0:T(8,128)}, f32[12,1152]{1,0:T(8,128)}, f32[12,384]{1,0:T(8,128)}, f32[1,12]{1,0:T(1,128)}) custom-call(bf16[1,2,288,384]{3,2,1,0:T(8,128)(2,1)} %get-tuple-element.12.grad_in, bf16[8,48,384]{2,1,0:T(8,128)(2,1)} %get-tuple-element.13.totals), custom_call_target="tpu_custom_call" | custom-call | tf_op jit(solution)/shard_map/pallas_call | solution.py:719

commit v2 on v1

--- a/solution.py
+++ b/solution.py
@@ -127,8 +127,26 @@
 
 
 def picks(target, rows, columns):
-    row, col = iotas(rows, columns)
-    return jnp.where(col == target(row), 1.0, 0.0).astype(BF16)
+    width = min(columns, 128)
+    row, col = iotas(rows, width)
+    lane = target(row) - col
+    parts = [
+        jnp.where(lane == first, 1.0, 0.0).astype(BF16)
+        for first in range(0, columns // width * width, width)
+    ]
+    rest = columns - columns // width * width
+    if rest:
+        last = lane[:, 0:rest] == columns - rest
+        parts.append(jnp.where(last, 1.0, 0.0).astype(BF16))
+    return parts[0] if len(parts) == 1 else jnp.concatenate(parts, 1)
+
+
+def wrap(n, size):
+    return jnp.where(n >= size, n - size, n)
+
+
+def upper(x):
+    return jnp.where(x >= 2, 1, 0)
 
 
 class Place:
@@ -141,12 +159,12 @@
         self.rail = self.low * 2 + self.core
 
     def at(self, dx=0, dy=0, dz=0, other=False):
-        x, y, z = lax.rem(self.x + dx, 4), lax.rem(self.y + dy, 8), lax.rem(self.z + dz, 8)
+        x, y, z = wrap(self.x + dx, 4), wrap(self.y + dy, 8), wrap(self.z + dz, 8)
         core = 1 - self.core if other else self.core
-        return (lax.div(x, 2) * 8 + y, z * 4 + lax.rem(x, 2) * 2 + core)
+        return (upper(x) * 8 + y, z * 4 + (x - upper(x) * 2) * 2 + core)
 
     def peer(self, k):
-        return (self.clip, lax.rem(self.tm + k, WAYS))
+        return (self.clip, wrap(self.tm + k, WAYS))
 
 
 def greet(me, outer):
@@ -178,61 +196,13 @@
     pltpu.make_async_copy(ref, ref, sem).wait()
 
 
-def each_peer(act, first=0, last=WAYS - 1):
-    def step(i, carry):
-        act(lax.rem(i + 12, WAYS - 1) + 1)
+def each_peer(act):
+    def step(k, carry):
+        act(k)
         return carry
 
-    lax.fori_loop(first, last, step, 0)
-
-
-class Exchange:
-    def __init__(self, me, src, dst, cuts, sems, hops, hop_sems):
-        self.__dict__.update(locals())
-
-    def send(self, part, k):
-        me, rows = self.me, pl.ds(*self.cuts[part])
-        device = me.peer(k)
-        target = device[1]
-        opposite = lax.rem(me.z + 4, 8) == lax.div(target, 4)
-        over = opposite & (lax.rem(target, 2) != me.core)
-        piece = self.src.at[target, rows]
-
-        @pl.when(over)
-        def _():
-            slot = self.hops.at[part, lax.rem(lax.div(target, 2), 2), pl.ds(0, self.cuts[part][1])]
-            pltpu.make_async_remote_copy(
-                src_ref=piece, dst_ref=slot, send_sem=self.sems[0].at[part],
-                recv_sem=self.hop_sems[1].at[part], device_id=me.at(dz=6), device_id_type=MESH,
-            ).start()
-
-        @pl.when(jnp.logical_not(over))
-        def _():
-            remote(piece, self.dst.at[me.tm, rows], self.sems, part, device).start()
-
-    def forward(self, part):
-        me, size = self.me, self.cuts[part][1]
-        self.settle_hops(part, self.hop_sems[1])
-        source, target = me.at(dz=2)[1], me.at(dz=6, other=True)
-        for low in range(2):
-            device = (target[0], lax.div(target[1], 4) * 4 + low * 2 + 1 - me.core)
-            pltpu.make_async_remote_copy(
-                src_ref=self.hops.at[part, low, pl.ds(0, size)],
-                dst_ref=self.dst.at[source, pl.ds(*self.cuts[part])],
-                send_sem=self.hop_sems[0].at[part], recv_sem=self.sems[1].at[part],
-                device_id=device, device_id_type=MESH,
-            ).start()
-
-    def settle_hops(self, part, sems):
-        settle(self.hops.at[part, :, pl.ds(0, self.cuts[part][1])], sems.at[part])
-
-    def arrive(self, part):
-        settle(self.dst.at[pl.ds(0, WAYS - 1), pl.ds(*self.cuts[part])], self.sems[1].at[part])
-
-    def drain(self):
-        for part in range(2):
-            settle(self.src.at[pl.ds(0, WAYS - 1), pl.ds(*self.cuts[part])], self.sems[0].at[part])
-            self.settle_hops(part, self.hop_sems[0])
+    lax.fori_loop(13, WAYS, step, 0)
+    lax.fori_loop(1, 13, step, 0)
 
 
 def pack_in(d, video, cot, out):
@@ -286,20 +256,22 @@
 
 
 def unpack_weights(weights, w, gain):
-    for m in range(MATS + 1):
-        h, j = m // 4, m % 4
+    for j in range(4):
         base, size = ((0, 16), (0, 32), (16, 32), (32, 16))[j]
 
         def column(r):
             block = twelfth(r)
             return ((block & 3) * 8 + (block >> 2)) * size + (r - block * SHARE) + j * SHARE - base
 
-        source = weights[h, :, :, base : base + size, :].reshape(WAYS * size, C)
-        got = mm(picks(column, C, WAYS * size), source)
-        if m < MATS:
-            w[:, m * C : (m + 1) * C] = got.astype(BF16)
-        else:
-            gain[...] = jnp.sum(got, axis=0, keepdims=True)
+        pick = picks(column, C, WAYS * size)
+        for h in range(2):
+            m = 4 * h + j
+            source = weights[h, :, :, base : base + size, :].reshape(WAYS * size, C)
+            got = mm(pick, source)
+            if m < MATS:
+                w[:, m * C : (m + 1) * C] = got.astype(BF16)
+            else:
+                gain[...] = jnp.sum(got, axis=0, keepdims=True)
 
 
 def pack_out(part, gv, out):
@@ -347,7 +319,7 @@
         return copy
 
     def block(dz, *rows):
-        return weights.at[half, me.rail, lax.rem(me.z + dz, 8), *rows]
+        return weights.at[half, me.rail, wrap(me.z + dz, 8), *rows]
 
     def over_z():
         for k in (2, 6, 1, 7):
@@ -403,7 +375,7 @@
         self.mine = lax.div(me.x, 2)
 
     def to_core(self, r, i):
-        slot = lax.rem(self.me.core + 1 + r, 2) + 2 * i
+        slot = (self.me.core if r else 1 - self.me.core) + 2 * i
         return remote(
             self.sums.at[r, slot], self.core_in.at[r, i], self.sems["c"], 2 * r + i,
             self.me.at(other=True),
@@ -415,14 +387,14 @@
 
     def to_owner(self, r, i):
         step = 3 if i else 1
-        which = lax.div(lax.rem(self.me.x + step, 4), 2)
+        which = upper(wrap(self.me.x + step, 4))
         copy = remote(
             self.held.at[r, which], self.x_in.at[i], self.sems["x"], 2 * r + i, self.me.at(dx=step)
         )
         return which, copy
 
     def over_z(self, k):
-        first = pl.multiple_of(lax.rem(self.me.z + k, 8) * QUAD, QUAD)
+        first = pl.multiple_of(wrap(self.me.z + k, 8) * QUAD, QUAD)
         part = self.held.at[self.round, self.mine, pl.ds(first, QUAD)]
         return remote(part, self.z_in.at[k], self.sems["z"], 0, self.me.at(dz=k))
 
@@ -447,7 +419,7 @@
     def core_add(self, r):
         for i in range(2):
             self.to_core(r, i).wait_recv()
-            slot = lax.rem(self.me.core + r, 2) + 2 * i
+            slot = (1 - self.me.core if r else self.me.core) + 2 * i
             both = self.sums[r, slot].astype(F32) + self.core_in[r, i].astype(F32)
             self.held[r, i] = both.astype(BF16)
 
@@ -523,11 +495,11 @@
 def main_kernel(
     video_in, cot_in, conv_in, qkv_in, out_in, gain_in, grad_video, totals,
     video, cotangent, conv, qkv, out_w, parcels, shard, landed, weights,
-    w, gain, parcels_out, landed_out, hops_in, hops_out, acc, gain_acc,
+    w, gain, parcels_out, landed_out, acc, gain_acc,
     x, cot, s1, s2, hidden, inverse, normed, packed, attended, grad_att, grad_packed,
     grad_hidden, a1, a2, gv,
     sums, core_in, held, mid, x_in, z_in, y_in, y_out,
-    l_s, i_s, i_r, o_s, o_r, h_s, h_r, g_s, g_r, wz_s, wz_r, wy_s, wy_r, wx_s, wx_r, wc_s, wc_r,
+    l_s, i_s, i_r, o_s, o_r, wz_s, wz_r, wy_s, wy_r, wx_s, wx_r, wc_s, wc_r,
     sc_s, sc_r, sm_s, sm_r, sx_s, sx_r, sz_s, sz_r, sy_s, sy_r, sf_s, sf_r,
 ):
     me = Place()
@@ -551,22 +523,38 @@
     )
     over_z()
 
-    coming = Exchange(me, parcels, landed, CUTS, (i_s, i_r), hops_in, (h_s, h_r))
-    going = Exchange(
-        me, parcels_out, landed_out, ((0, 32), (32, 32)), (o_s, o_r), hops_out, (g_s, g_r)
-    )
-
-    def pack_and_send(k):
-        pack_in(me.peer(k)[1], video, cotangent, parcels)
-        coming.send(0, k)
-
-    each_peer(pack_and_send, 0, 10)
+    def coming(part, k):
+        device, rows = me.peer(k), pl.ds(*CUTS[part])
+        return remote(
+            parcels.at[device[1], rows], landed.at[me.tm, rows], (i_s, i_r), part, device
+        )
+
+    def going(part, k):
+        device, rows = me.peer(k), pl.ds(32 * part, 32)
+        return remote(
+            parcels_out.at[device[1], rows], landed_out.at[me.tm, rows], (o_s, o_r), part, device
+        )
+
+    def arrive(part, sems):
+        settle(landed.at[pl.ds(0, WAYS - 1), pl.ds(*CUTS[part])], sems.at[part])
+
+    def returned(part, sems):
+        settle(landed_out.at[pl.ds(0, WAYS - 1), pl.ds(32 * part, 32)], sems.at[part])
+
+    def two(i, carry):
+        pack_in(me.peer(2 * i)[1], video, cotangent, parcels)
+        pack_in(me.peer(2 * i + 1)[1], video, cotangent, parcels)
+        coming(0, 2 * i).start()
+        coming(0, 2 * i + 1).start()
+        return carry
+
+    lax.fori_loop(7, 16, two, 0)
     onward()
-    each_peer(pack_and_send, 10)
-    coming.forward(0)
+    lax.fori_loop(1, 7, two, 0)
+    pack_in(me.peer(1)[1], video, cotangent, parcels)
+    coming(0, 1).start()
     pack_in(me.tm, video, cotangent, landed)
-    rest(lambda: each_peer(lambda k: coming.send(1, k)))
-    coming.forward(1)
+    rest(lambda: each_peer(lambda k: coming(1, k).start()))
     unpack_weights(weights, w, gain)
 
     total = Sums(
@@ -587,28 +575,26 @@
             pgrad_packed, pgrad_hidden, pa1, pa2, pgv,
         ) = (ref.at[rows] for ref in tall)
         blocks = BLOCKS[part]
-        coming.arrive(part)
+        arrive(part, i_r)
         unpack_in(part, landed, px, pcot)
-        if part == 1:
-            going.forward(0)
         forward(blocks, w, gain, px, ps1, ps2, phidden, pinverse, pnormed, ppacked)
         attention(blocks, w, pcot, ppacked, pattended, pgrad_att, pgrad_packed)
 
-        def add(n, left, right):
-            product = mm_tn(left, right)
+        def add(n, product):
             if part == 0:
                 acc[n] = product
             else:
                 sums[n // 4, n % 4] = (acc[n] + product).astype(BF16)
 
         def early_sums():
-            add(0, pattended[...], pcot[...])
+            add(0, mm_tn(pattended[...], pcot[...]))
+            product = mm_tn(pnormed[...], pgrad_packed[...])
             for i in range(3):
-                add(1 + i, pnormed[...], pgrad_packed[:, i * C : (i + 1) * C])
+                add(1 + i, product[:, i * C : (i + 1) * C])
 
         def late_sums():
             for tap, ref in enumerate((px, ps1, ps2)):
-                add(4 + tap, ref[...], pgrad_hidden[...])
+                add(4 + tap, mm_tn(ref[...], pgrad_hidden[...]))
 
         def send_back():
             pack_out(part, pgv, parcels_out)
@@ -623,7 +609,7 @@
             gain_acc[...] = norm_back()
             conv_back(blocks, w, pgrad_hidden, pa1, pa2, pgv)
             send_back()
-            each_peer(lambda k: going.send(0, k))
+            each_peer(lambda k: going(0, k).start())
             early_sums()
             late_sums()
         else:
@@ -640,22 +626,22 @@
             total.core_add(1)
             send_back()
             total.own_x(0)
-            each_peer(lambda k: going.send(1, k))
+            each_peer(lambda k: going(1, k).start())
     total.relay(1)
     total.own_x(1)
-    going.forward(1)
     total.own_z()
     for part in range(2):
-        going.arrive(part)
+        returned(part, o_r)
     unpack_out(landed_out, grad_video)
     total.own_y()
     total.drain()
     drain()
-    coming.drain()
-    going.drain()
-
-
-def call(kernel, outs, scratch, places, out_places, collective=None):
+    for part in range(2):
+        arrive(part, i_s)
+        returned(part, o_s)
+
+
+def call(kernel, outs, scratch, places, out_places, mib, collective=None):
     extra = {} if collective is None else dict(collective_id=collective, has_side_effects=True)
     return pl.pallas_call(
         kernel,
@@ -663,7 +649,7 @@
         in_specs=[pl.BlockSpec(memory_space=place) for place in places],
         out_specs=[pl.BlockSpec(memory_space=place) for place in out_places],
         scratch_shapes=scratch,
-        compiler_params=pltpu.CompilerParams(vmem_limit_bytes=56 * 1024 * 1024, **extra),
+        compiler_params=pltpu.CompilerParams(vmem_limit_bytes=mib * 1024 * 1024, **extra),
     )
 
 
@@ -675,24 +661,22 @@
     scratch = [
         held(1, 2, 288, C), held(1, 2, 288, C), held(3, SHARE, C), held(SHARE, 3 * C), held(SHARE, C),
         held(WAYS, PIECE, 128), held(2, QUAD, C), held(WAYS, PIECE, 128), held(2, 4, 8, QUAD, C),
-        held(C, WIDE), held(1, C, kind=F32), held(WAYS, BACK, 128), held(WAYS, BACK, 128),
-        held(2, 2, 64, 128), held(2, 2, 32, 128), held(MATS, C, C, kind=F32),
+        held(C, WIDE), held(1, C, kind=F32), held(WAYS, BACK, 128), held(WAYS, BACK, 128), held(MATS, C, C, kind=F32),
         held(1, C, kind=F32),
         tall, tall, tall, tall, tall, held(ROWS, 1, kind=F32), tall, held(ROWS, 3 * C), tall, tall,
         held(ROWS, 3 * C), tall, tall, tall, tall,
         held(2, 4, C, C), held(2, 2, C, C), held(2, 2, C, C), held(2, HALF, C), held(2, C, C),
         held(8, QUAD, C), held(8, QUAD, C), held(QUAD, C),
     ]
-    counts = [5] + [2] * 8 + [8, 8, 2, 2, 4, 4, 8, 8] + [4] * 6 + [1] * 6
+    counts = [5] + [2] * 4 + [8, 8, 2, 2, 4, 4, 8, 8] + [4] * 6 + [1] * 6
     scratch += [pltpu.SemaphoreType.DMA((n,)) for n in counts]
     outs = [(args[0].shape, BF16), ((8, QUAD, C), BF16)]
     places = [pl.ANY] * 5 + [pltpu.VMEM]
-    return call(main_kernel, outs, scratch, places, [pltpu.VMEM] * 2, 1)(*args)
-
-
-def finish_kernel(factor, grad_in, totals, grad_video, conv, qkv, out_w, gain, sem):
-    copy = pltpu.make_async_copy(grad_in, grad_video, sem)
-    copy.start()
+    return call(main_kernel, outs, scratch, places, [pltpu.VMEM] * 2, 56, 1)(*args)
+
+
+def finish_kernel(factor, grad_in, totals, grad_video, conv, qkv, out_w, gain):
+    grad_video[...] = grad_in[...]
     tm = lax.axis_index("tm")
     pick = picks(lambda r: r + lax.rem(tm, 4) * SHARE, 16, QUAD)
     got = [mm(pick, totals[m]) for m in range(8)]
@@ -704,7 +688,6 @@
     line = mm(got[7].astype(BF16), jnp.where(row == tm * SHARE + col, 1.0, 0.0).astype(BF16))
     row, col = iotas(16, SHARE)
     gain[...] = jnp.sum(jnp.where(row == col, line, 0.0), axis=0, keepdims=True) * factor
-    copy.wait()
 
 
 def body(video, conv_w, qkv_w, out_w, gain, cotangent):
@@ -717,8 +700,7 @@
         ((1, SHARE), F32),
     ]
     got = call(
-        functools.partial(finish_kernel, factor), outs, [pltpu.SemaphoreType.DMA],
-        [pltpu.VMEM] * 2, [pl.ANY] + [pltpu.VMEM] * 4,
+        functools.partial(finish_kernel, factor), outs, [], [pltpu.VMEM] * 2, [pltpu.VMEM] * 5, 8
     )(grad_video, totals)
     return (*got[:4], got[4].reshape(SHARE))
 

time: 106 us -> 102 us (0.962)
  Pallas kernels: 105 us -> 98.8 us
  local copies, waits for them, and re-layouts: 0 us -> 1.97 us
    pallas_call x2, Pallas kernels: 105 us -> 98.8 us  [the longest x1 97.9 us: main(): call(main_kernel, outs, scratch, places, [pltpu.VMEM] * 2, 56, 1)(*args)]
    unnamed x0 -> x4, local copies, waits for them, and re-layouts: none -> 1.97 us
where the time goes in v2:
time: 102 us; the launch traced here: 101 us
  Pallas kernels  98.8 us (97%)
  local copies, waits for them, and re-layouts  1.97 us (2%)
    pallas_call x1, Pallas kernels, main(): call(main_kernel, outs, scratch, places, [pltpu.VMEM] * 2, 56, 1)(*args)  97.9 us

profile of v2, /device:TPU:1, one launch (start us, length us, event | category | flops | bytes accessed | tf_op | source)
XLA Modules:
  0.0 101.5 jit_solution(17015823305405293967)
XLA Ops:
  0.6 97.9 %shard_map.101 = (bf16[1,2,288,384]{3,2,1,0:T(8,128)(2,1)}, bf16[8,48,384]{2,1,0:T(8,128)(2,1)}) custom-call(bf16[1,2,288,384]{3,2,1,0:T(8,128)(2,1)} %video_in.1, bf16[1,2,288,384]{3,2,1,0:T(8,128)(2,1)} %cot_in.1, bf16[3,12,384]{2,1,0:T(8,128)(2,1)} %conv_in.1, bf16[12,1152]{1,0:T(8,128)(2,1)} %qkv_in.1, bf16[12,384]{1,0:T(8,128)(2,1)} %out_in.1, ...), custom_call_target="tpu_custom_call" | custom-call | tf_op jit(solution)/shard_map/pallas_call | solution.py:675
  98.5 0.0 copy-start
  98.5 1.0 copy-done
  99.5 0.0 copy-start.1
  99.5 1.0 copy-done.1
  100.5 1.0 shard_map.102
Async XLA Ops:
  98.5 1.0 copy-start
  99.5 1.0 copy-start.1

commit v3 on v2

--- a/solution.py
+++ b/solution.py
@@ -197,12 +197,13 @@
 
 
 def each_peer(act):
-    def step(k, carry):
-        act(k)
+    def step(i, carry):
+        act(16 - i)
+        act(16 + i)
         return carry
 
-    lax.fori_loop(13, WAYS, step, 0)
-    lax.fori_loop(1, 13, step, 0)
+    act(16)
+    lax.fori_loop(1, 16, step, 0)
 
 
 def pack_in(d, video, cot, out):
@@ -542,17 +543,17 @@
         settle(landed_out.at[pl.ds(0, WAYS - 1), pl.ds(32 * part, 32)], sems.at[part])
 
     def two(i, carry):
-        pack_in(me.peer(2 * i)[1], video, cotangent, parcels)
-        pack_in(me.peer(2 * i + 1)[1], video, cotangent, parcels)
-        coming(0, 2 * i).start()
-        coming(0, 2 * i + 1).start()
+        for k in (16 - i, 16 + i):
+            pack_in(me.peer(k)[1], video, cotangent, parcels)
+        for k in (16 - i, 16 + i):
+            coming(0, k).start()
         return carry
 
-    lax.fori_loop(7, 16, two, 0)
+    pack_in(me.peer(16)[1], video, cotangent, parcels)
+    coming(0, 16).start()
+    lax.fori_loop(1, 6, two, 0)
     onward()
-    lax.fori_loop(1, 7, two, 0)
-    pack_in(me.peer(1)[1], video, cotangent, parcels)
-    coming(0, 1).start()
+    lax.fori_loop(6, 16, two, 0)
     pack_in(me.tm, video, cotangent, landed)
     rest(lambda: each_peer(lambda k: coming(1, k).start()))
     unpack_weights(weights, w, gain)
@@ -675,8 +676,17 @@
     return call(main_kernel, outs, scratch, places, [pltpu.VMEM] * 2, 56, 1)(*args)
 
 
-def finish_kernel(factor, grad_in, totals, grad_video, conv, qkv, out_w, gain):
-    grad_video[...] = grad_in[...]
+def finish_kernel(
+    factor, grad_in, totals_in, grad_video, conv, qkv, out_w, gain, grad, totals, sems
+):
+    come = pltpu.make_async_copy(grad_in, grad, sems.at[0])
+    come.start()
+    read = pltpu.make_async_copy(totals_in, totals, sems.at[1])
+    read.start()
+    come.wait()
+    go = pltpu.make_async_copy(grad, grad_video, sems.at[2])
+    go.start()
+    read.wait()
     tm = lax.axis_index("tm")
     pick = picks(lambda r: r + lax.rem(tm, 4) * SHARE, 16, QUAD)
     got = [mm(pick, totals[m]) for m in range(8)]
@@ -688,6 +698,7 @@
     line = mm(got[7].astype(BF16), jnp.where(row == tm * SHARE + col, 1.0, 0.0).astype(BF16))
     row, col = iotas(16, SHARE)
     gain[...] = jnp.sum(jnp.where(row == col, line, 0.0), axis=0, keepdims=True) * factor
+    go.wait()
 
 
 def body(video, conv_w, qkv_w, out_w, gain, cotangent):
@@ -700,7 +711,12 @@
         ((1, SHARE), F32),
     ]
     got = call(
-        functools.partial(finish_kernel, factor), outs, [], [pltpu.VMEM] * 2, [pltpu.VMEM] * 5, 8
+        functools.partial(finish_kernel, factor), outs,
+        [
+            pltpu.VMEM(video.shape, BF16), pltpu.VMEM((8, QUAD, C), BF16),
+            pltpu.SemaphoreType.DMA((3,)),
+        ],
+        [pl.ANY] * 2, [pl.ANY] + [pltpu.VMEM] * 4, 56,
     )(grad_video, totals)
     return (*got[:4], got[4].reshape(SHARE))
 

time: 102 us -> 100 us (0.980)
  local copies, waits for them, and re-layouts: 1.97 us -> 0 us
    unnamed x4 -> x0, local copies, waits for them, and re-layouts: 1.97 us -> none
    pallas_call x1, Pallas kernels: 1 us -> 2.46 us  [body(): call(functools.partial(finish_kernel, factor), outs, [pltpu.VMEM(video.sh...]
where the time goes in v3:
time: 100 us
  Pallas kernels  99.5 us (100%)
    pallas_call x1, Pallas kernels, main(): call(main_kernel, outs, scratch, places, [pltpu.VMEM] * 2, 56, 1)(*args)  97 us
    pallas_call x1, Pallas kernels, body(): call(functools.partial(finish_kernel, factor), outs, [pltpu.VMEM(video.sh...  2.46 us

profile of v3, /device:TPU:1, one launch (start us, length us, event | category | flops | bytes accessed | tf_op | source)
XLA Modules:
  0.0 100.3 jit_solution(768683289776343759)
XLA Ops:
  0.6 97.0 %shard_map.101 = (bf16[1,2,288,384]{3,2,1,0:T(8,128)(2,1)}, bf16[8,48,384]{2,1,0:T(8,128)(2,1)}) custom-call(bf16[1,2,288,384]{3,2,1,0:T(8,128)(2,1)} %video_in.1, bf16[1,2,288,384]{3,2,1,0:T(8,128)(2,1)} %cot_in.1, bf16[3,12,384]{2,1,0:T(8,128)(2,1)} %conv_in.1, bf16[12,1152]{1,0:T(8,128)(2,1)} %qkv_in.1, bf16[12,384]{1,0:T(8,128)(2,1)} %out_in.1, ...), custom_call_target="tpu_custom_call" | custom-call | tf_op jit(solution)/shard_map/pallas_call | solution.py:676
  97.6 2.5 %shard_map.102 = (bf16[1,2,288,384]{3,2,1,0:T(8,128)(2,1)}, f32[3,12,384]{2,1,0:T(8,128)}, f32[12,1152]{1,0:T(8,128)}, f32[12,384]{1,0:T(8,128)}, f32[1,12]{1,0:T(1,128)}) custom-call(bf16[1,2,288,384]{3,2,1,0:T(8,128)(2,1)} %get-tuple-element.12.grad_in, bf16[8,48,384]{2,1,0:T(8,128)(2,1)} %get-tuple-element.13.totals_in), custom_call_target="tpu_custom_call" | custom-call | tf_op jit(solution)/shard_map/pallas_call | solution.py:713

commit v4 on v3

--- a/solution.py
+++ b/solution.py
@@ -196,14 +196,15 @@
     pltpu.make_async_copy(ref, ref, sem).wait()
 
 
-def each_peer(act):
+def each_peer(act, first=0, last=16):
     def step(i, carry):
         act(16 - i)
         act(16 + i)
         return carry
 
-    act(16)
-    lax.fori_loop(1, 16, step, 0)
+    if first == 0:
+        act(16)
+    lax.fori_loop(max(first, 1), last, step, 0)
 
 
 def pack_in(d, video, cot, out):
@@ -336,7 +337,7 @@
         go(remote(block(6), block(6), z_sems, 3, me.at(dz=1)))
         go(remote(block(2), block(2), z_sems, 5, me.at(dz=7)))
 
-    def rest(between):
+    def rest(after):
         for copy in begun[2:]:
             copy.wait_recv()
         beyond = (1 - me.low) * 2 + me.core
@@ -349,7 +350,6 @@
             mine = part(half, me.rail, i)
             xs.append(go(remote(mine, mine, x_sems, i, me.at(dx=step))))
             cs.append(go(remote(mine, mine, c_sems, i, me.at(other=True))))
-        between()
         for i, step in ((0, 1), (1, 3)):
             ys[i].wait_recv()
             mine = part(1 - half, me.rail, i)
@@ -359,6 +359,7 @@
             xs[n].wait_recv()
             mine = part(half if n < 2 else 1 - half, beyond, n % 2)
             cs.append(go(remote(mine, mine, c_sems, 4 + n, me.at(other=True))))
+        after()
         for copy in cs:
             copy.wait_recv()
 
@@ -627,14 +628,15 @@
             total.core_add(1)
             send_back()
             total.own_x(0)
-            each_peer(lambda k: going(1, k).start())
     total.relay(1)
     total.own_x(1)
+    each_peer(lambda k: going(1, k).start(), 0, 8)
     total.own_z()
+    each_peer(lambda k: going(1, k).start(), 8, 16)
+    total.own_y()
     for part in range(2):
         returned(part, o_r)
     unpack_out(landed_out, grad_video)
-    total.own_y()
     total.drain()
     drain()
     for part in range(2):

time: 100 us -> 96.4 us (0.964)
  Pallas kernels: 99.5 us -> 95.5 us
    pallas_call x1, Pallas kernels: 97 us -> 93 us  [main(): call(main_kernel, outs, scratch, places, [pltpu.VMEM] * 2, 56, 1)(*args)]
where the time goes in v4:
time: 96.4 us; the launch traced here: 96.3 us
  Pallas kernels  95.5 us (99%)
    pallas_call x1, Pallas kernels, main(): call(main_kernel, outs, scratch, places, [pltpu.VMEM] * 2, 56, 1)(*args)  93 us
    pallas_call x1, Pallas kernels, body(): call(functools.partial(finish_kernel, factor), outs, [pltpu.VMEM(video.sh...  2.46 us

profile of v4, /device:TPU:1, one launch (start us, length us, event | category | flops | bytes accessed | tf_op | source)
XLA Modules:
  0.0 96.3 jit_solution(4769335440399906783)
XLA Ops:
  0.6 93.0 %shard_map.101 = (bf16[1,2,288,384]{3,2,1,0:T(8,128)(2,1)}, bf16[8,48,384]{2,1,0:T(8,128)(2,1)}) custom-call(bf16[1,2,288,384]{3,2,1,0:T(8,128)(2,1)} %video_in.1, bf16[1,2,288,384]{3,2,1,0:T(8,128)(2,1)} %cot_in.1, bf16[3,12,384]{2,1,0:T(8,128)(2,1)} %conv_in.1, bf16[12,1152]{1,0:T(8,128)(2,1)} %qkv_in.1, bf16[12,384]{1,0:T(8,128)(2,1)} %out_in.1, ...), custom_call_target="tpu_custom_call" | custom-call | tf_op jit(solution)/shard_map/pallas_call | solution.py:678
  93.6 2.5 %shard_map.102 = (bf16[1,2,288,384]{3,2,1,0:T(8,128)(2,1)}, f32[3,12,384]{2,1,0:T(8,128)}, f32[12,1152]{1,0:T(8,128)}, f32[12,384]{1,0:T(8,128)}, f32[1,12]{1,0:T(1,128)}) custom-call(bf16[1,2,288,384]{3,2,1,0:T(8,128)(2,1)} %get-tuple-element.12.grad_in, bf16[8,48,384]{2,1,0:T(8,128)(2,1)} %get-tuple-element.13.totals_in), custom_call_target="tpu_custom_call" | custom-call | tf_op jit(solution)/shard_map/pallas_call | solution.py:715

commit v5 on v4

--- a/solution.py
+++ b/solution.py
@@ -337,29 +337,39 @@
         go(remote(block(6), block(6), z_sems, 3, me.at(dz=1)))
         go(remote(block(2), block(2), z_sems, 5, me.at(dz=7)))
 
-    def rest(after):
-        for copy in begun[2:]:
+    beyond = (1 - me.low) * 2 + me.core
+    ways = ((0, 1, 1), (1, 7, 3))
+    ys, xs, cs = [], [], []
+
+    def part(h, rail, i):
+        return weights.at[h, rail, pl.ds(4 * i, 4)]
+
+    def over_x(h, n, i, step):
+        mine = part(h, me.rail, i)
+        xs.append(go(remote(mine, mine, x_sems, n, me.at(dx=step))))
+        cs.append(go(remote(mine, mine, c_sems, n, me.at(other=True))))
+
+    def own_half():
+        for copy in list(begun[2:]):
             copy.wait_recv()
-        beyond = (1 - me.low) * 2 + me.core
-        part = lambda h, rail, i: weights.at[h, rail, pl.ds(4 * i, 4)]
-        ys, xs, cs = [], [], []
-        for i, step in ((0, 1), (1, 7)):
+        for i, up, _ in ways:
             mine = part(half, me.rail, i)
-            ys.append(go(remote(mine, mine, y_sems, i, me.at(dy=step))))
-        for i, step in ((0, 1), (1, 3)):
-            mine = part(half, me.rail, i)
-            xs.append(go(remote(mine, mine, x_sems, i, me.at(dx=step))))
-            cs.append(go(remote(mine, mine, c_sems, i, me.at(other=True))))
-        for i, step in ((0, 1), (1, 3)):
+            ys.append(go(remote(mine, mine, y_sems, i, me.at(dy=up))))
+        for i, _, side in ways:
+            over_x(half, i, i, side)
+
+    def other_half():
+        for i, _, side in ways:
             ys[i].wait_recv()
-            mine = part(1 - half, me.rail, i)
-            xs.append(go(remote(mine, mine, x_sems, 2 + i, me.at(dx=step))))
-            cs.append(go(remote(mine, mine, c_sems, 2 + i, me.at(other=True))))
+            over_x(1 - half, 2 + i, i, side)
+
+    def far_rail():
         for n in range(4):
             xs[n].wait_recv()
             mine = part(half if n < 2 else 1 - half, beyond, n % 2)
             cs.append(go(remote(mine, mine, c_sems, 4 + n, me.at(other=True))))
-        after()
+
+    def done():
         for copy in cs:
             copy.wait_recv()
 
@@ -367,7 +377,7 @@
         for copy in begun:
             copy.wait_send()
 
-    return over_z, onward, rest, drain
+    return (over_z, onward, own_half, other_half, far_rail, done), drain
 
 
 class Sums:
@@ -520,10 +530,10 @@
         copy.wait()
     met()
 
-    over_z, onward, rest, drain = gather_weights(
+    steps, drain = gather_weights(
         me, shard, weights, (wz_s, wz_r), (wy_s, wy_r), (wx_s, wx_r), (wc_s, wc_r)
     )
-    over_z()
+    steps[0]()
 
     def coming(part, k):
         device, rows = me.peer(k), pl.ds(*CUTS[part])
@@ -552,11 +562,17 @@
 
     pack_in(me.peer(16)[1], video, cotangent, parcels)
     coming(0, 16).start()
-    lax.fori_loop(1, 6, two, 0)
-    onward()
-    lax.fori_loop(6, 16, two, 0)
+    lax.fori_loop(1, 4, two, 0)
+    steps[1]()
+    lax.fori_loop(4, 7, two, 0)
+    steps[2]()
+    lax.fori_loop(7, 12, two, 0)
+    steps[3]()
+    lax.fori_loop(12, 16, two, 0)
     pack_in(me.tm, video, cotangent, landed)
-    rest(lambda: each_peer(lambda k: coming(1, k).start()))
+    steps[4]()
+    each_peer(lambda k: coming(1, k).start())
+    steps[5]()
     unpack_weights(weights, w, gain)
 
     total = Sums(
@@ -624,11 +640,11 @@
             total.core_send(1)
             total.core_add(0)
             conv_back(blocks, w, pgrad_hidden, pa1, pa2, pgv)
+            total.core_add(1)
             total.relay(0)
-            total.core_add(1)
             send_back()
-            total.own_x(0)
     total.relay(1)
+    total.own_x(0)
     total.own_x(1)
     each_peer(lambda k: going(1, k).start(), 0, 8)
     total.own_z()

time: 96.4 us -> 95.7 us (level)
  no operation moved by 1% of the time
where the time goes in v5:
time: 95.7 us; the launch traced here: 95.5 us
  Pallas kernels  94.7 us (99%)
    pallas_call x1, Pallas kernels, main(): call(main_kernel, outs, scratch, places, [pltpu.VMEM] * 2, 56, 1)(*args)  92.2 us
    pallas_call x1, Pallas kernels, body(): call(functools.partial(finish_kernel, factor), outs, [pltpu.VMEM(video.sh...  2.46 us

profile of v5, /device:TPU:1, one launch (start us, length us, event | category | flops | bytes accessed | tf_op | source)
XLA Modules:
  0.0 95.5 jit_solution(16812503165219661503)
XLA Ops:
  0.6 92.2 %shard_map.101 = (bf16[1,2,288,384]{3,2,1,0:T(8,128)(2,1)}, bf16[8,48,384]{2,1,0:T(8,128)(2,1)}) custom-call(bf16[1,2,288,384]{3,2,1,0:T(8,128)(2,1)} %video_in.1, bf16[1,2,288,384]{3,2,1,0:T(8,128)(2,1)} %cot_in.1, bf16[3,12,384]{2,1,0:T(8,128)(2,1)} %conv_in.1, bf16[12,1152]{1,0:T(8,128)(2,1)} %qkv_in.1, bf16[12,384]{1,0:T(8,128)(2,1)} %out_in.1, ...), custom_call_target="tpu_custom_call" | custom-call | tf_op jit(solution)/shard_map/pallas_call | solution.py:694
  92.9 2.5 %shard_map.102 = (bf16[1,2,288,384]{3,2,1,0:T(8,128)(2,1)}, f32[3,12,384]{2,1,0:T(8,128)}, f32[12,1152]{1,0:T(8,128)}, f32[12,384]{1,0:T(8,128)}, f32[1,12]{1,0:T(1,128)}) custom-call(bf16[1,2,288,384]{3,2,1,0:T(8,128)(2,1)} %get-tuple-element.12.grad_in, bf16[8,48,384]{2,1,0:T(8,128)(2,1)} %get-tuple-element.13.totals_in), custom_call_target="tpu_custom_call" | custom-call | tf_op jit(solution)/shard_map/pallas_call | solution.py:731

commit v6 on v5

--- a/solution.py
+++ b/solution.py
@@ -222,7 +222,7 @@
         return block * 32 + spot + shift
 
     pick = picks(column, PIECE, 384)
-    out[d] = mm(pick, jnp.concatenate(pieces, 0)).astype(BF16)
+    out[...] = mm(pick, jnp.concatenate(pieces, 0)).astype(BF16)
 
 
 def pack_weights(tm, conv, qkv, out_w, gain, shard):
@@ -511,12 +511,13 @@
     x, cot, s1, s2, hidden, inverse, normed, packed, attended, grad_att, grad_packed,
     grad_hidden, a1, a2, gv,
     sums, core_in, held, mid, x_in, z_in, y_in, y_out,
-    l_s, i_s, i_r, o_s, o_r, wz_s, wz_r, wy_s, wy_r, wx_s, wx_r, wc_s, wc_r,
+    l_s, v_s, v_r, i_s, i_r, o_s, o_r, wz_s, wz_r, wy_s, wy_r, wx_s, wx_r, wc_s, wc_r,
     sc_s, sc_r, sm_s, sm_r, sx_s, sx_r, sz_s, sz_r, sy_s, sy_r, sf_s, sf_r,
 ):
     me = Place()
     pairs = (
-        (conv_in, conv), (qkv_in, qkv), (out_in, out_w), (video_in, video), (cot_in, cotangent)
+        (conv_in, conv), (qkv_in, qkv), (out_in, out_w), (video_in, video.at[me.core]),
+        (cot_in, cotangent.at[me.core]),
     )
     reads = [pltpu.make_async_copy(src, dst, l_s.at[n]) for n, (src, dst) in enumerate(pairs)]
     for copy in reads:
@@ -529,16 +530,29 @@
     for copy in reads[3:]:
         copy.wait()
     met()
+    swaps = [
+        remote(ref.at[me.core], ref.at[me.core], (v_s, v_r), n, me.at(other=True))
+        for n, ref in enumerate((video, cotangent))
+    ]
+    for copy in swaps:
+        copy.start()
 
     steps, drain = gather_weights(
         me, shard, weights, (wz_s, wz_r), (wy_s, wy_r), (wx_s, wx_r), (wc_s, wc_r)
     )
     steps[0]()
 
+    chip = lax.div(me.tm, 2)
+
+    def toward(k):
+        there = wrap(chip + k, WAYS // 2)
+        return there, 2 * there + me.core
+
     def coming(part, k):
-        device, rows = me.peer(k), pl.ds(*CUTS[part])
+        (there, target), rows = toward(k), pl.ds(*CUTS[part])
         return remote(
-            parcels.at[device[1], rows], landed.at[me.tm, rows], (i_s, i_r), part, device
+            parcels.at[there, pl.ds(0, 2), rows], landed.at[pl.ds(2 * chip, 2), rows],
+            (i_s, i_r), part, (me.clip, target),
         )
 
     def going(part, k):
@@ -548,30 +562,45 @@
         )
 
     def arrive(part, sems):
-        settle(landed.at[pl.ds(0, WAYS - 1), pl.ds(*CUTS[part])], sems.at[part])
+        settle(landed.at[pl.ds(0, WAYS - 2), pl.ds(*CUTS[part])], sems.at[part])
 
     def returned(part, sems):
         settle(landed_out.at[pl.ds(0, WAYS - 1), pl.ds(32 * part, 32)], sems.at[part])
 
+    def pack(target, place):
+        for source in range(2):
+            pack_in(target, video.at[source], cotangent.at[source], place(source))
+
+    def one(k):
+        there, target = toward(k)
+        pack(target, lambda source: parcels.at[there, source])
+        coming(0, k).start()
+
     def two(i, carry):
-        for k in (16 - i, 16 + i):
-            pack_in(me.peer(k)[1], video, cotangent, parcels)
-        for k in (16 - i, 16 + i):
-            coming(0, k).start()
+        one(8 - i)
+        one(8 + i)
         return carry
 
-    pack_in(me.peer(16)[1], video, cotangent, parcels)
-    coming(0, 16).start()
-    lax.fori_loop(1, 4, two, 0)
+    for copy in swaps:
+        copy.wait_recv()
+    one(8)
+    lax.fori_loop(1, 2, two, 0)
     steps[1]()
-    lax.fori_loop(4, 7, two, 0)
+    lax.fori_loop(2, 4, two, 0)
     steps[2]()
-    lax.fori_loop(7, 12, two, 0)
+    lax.fori_loop(4, 6, two, 0)
     steps[3]()
-    lax.fori_loop(12, 16, two, 0)
-    pack_in(me.tm, video, cotangent, landed)
+    lax.fori_loop(6, 8, two, 0)
+    pack(me.tm, lambda source: landed.at[2 * chip + source])
     steps[4]()
-    each_peer(lambda k: coming(1, k).start())
+
+    def late(i, carry):
+        coming(1, 8 - i).start()
+        coming(1, 8 + i).start()
+        return carry
+
+    coming(1, 8).start()
+    lax.fori_loop(1, 8, late, 0)
     steps[5]()
     unpack_weights(weights, w, gain)
 
@@ -655,6 +684,8 @@
     unpack_out(landed_out, grad_video)
     total.drain()
     drain()
+    for copy in swaps:
+        copy.wait_send()
     for part in range(2):
         arrive(part, i_s)
         returned(part, o_s)
@@ -678,8 +709,8 @@
 
     tall = held(ROWS, C)
     scratch = [
-        held(1, 2, 288, C), held(1, 2, 288, C), held(3, SHARE, C), held(SHARE, 3 * C), held(SHARE, C),
-        held(WAYS, PIECE, 128), held(2, QUAD, C), held(WAYS, PIECE, 128), held(2, 4, 8, QUAD, C),
+        held(2, 1, 2, 288, C), held(2, 1, 2, 288, C), held(3, SHARE, C), held(SHARE, 3 * C), held(SHARE, C),
+        held(WAYS // 2, 2, PIECE, 128), held(2, QUAD, C), held(WAYS, PIECE, 128), held(2, 4, 8, QUAD, C),
         held(C, WIDE), held(1, C, kind=F32), held(WAYS, BACK, 128), held(WAYS, BACK, 128), held(MATS, C, C, kind=F32),
         held(1, C, kind=F32),
         tall, tall, tall, tall, tall, held(ROWS, 1, kind=F32), tall, held(ROWS, 3 * C), tall, tall,
@@ -687,7 +718,7 @@
         held(2, 4, C, C), held(2, 2, C, C), held(2, 2, C, C), held(2, HALF, C), held(2, C, C),
         held(8, QUAD, C), held(8, QUAD, C), held(QUAD, C),
     ]
-    counts = [5] + [2] * 4 + [8, 8, 2, 2, 4, 4, 8, 8] + [4] * 6 + [1] * 6
+    counts = [5] + [2] * 6 + [8, 8, 2, 2, 4, 4, 8, 8] + [4] * 6 + [1] * 6
     scratch += [pltpu.SemaphoreType.DMA((n,)) for n in counts]
     outs = [(args[0].shape, BF16), ((8, QUAD, C), BF16)]
     places = [pl.ANY] * 5 + [pltpu.VMEM]

time: 95.7 us -> 95.3 us (level)
  no operation moved by 1% of the time
where the time goes in v6:
time: 95.3 us; the launch traced here: 95.1 us
  Pallas kernels  94.3 us (99%)
    pallas_call x1, Pallas kernels, main(): call(main_kernel, outs, scratch, places, [pltpu.VMEM] * 2, 56, 1)(*args)  91.9 us
    pallas_call x1, Pallas kernels, body(): call(functools.partial(finish_kernel, factor), outs, [pltpu.VMEM(video.sh...  2.46 us

profile of v6, /device:TPU:1, one launch (start us, length us, event | category | flops | bytes accessed | tf_op | source)
XLA Modules:
  0.0 95.1 jit_solution(18137434413407391464)
XLA Ops:
  0.6 91.9 %shard_map.101 = (bf16[1,2,288,384]{3,2,1,0:T(8,128)(2,1)}, bf16[8,48,384]{2,1,0:T(8,128)(2,1)}) custom-call(bf16[1,2,288,384]{3,2,1,0:T(8,128)(2,1)} %video_in.1, bf16[1,2,288,384]{3,2,1,0:T(8,128)(2,1)} %cot_in.1, bf16[3,12,384]{2,1,0:T(8,128)(2,1)} %conv_in.1, bf16[12,1152]{1,0:T(8,128)(2,1)} %qkv_in.1, bf16[12,384]{1,0:T(8,128)(2,1)} %out_in.1, ...), custom_call_target="tpu_custom_call" | custom-call | tf_op jit(solution)/shard_map/pallas_call | solution.py:725
  92.5 2.5 %shard_map.102 = (bf16[1,2,288,384]{3,2,1,0:T(8,128)(2,1)}, f32[3,12,384]{2,1,0:T(8,128)}, f32[12,1152]{1,0:T(8,128)}, f32[12,384]{1,0:T(8,128)}, f32[1,12]{1,0:T(1,128)}) custom-call(bf16[1,2,288,384]{3,2,1,0:T(8,128)(2,1)} %get-tuple-element.12.grad_in, bf16[8,48,384]{2,1,0:T(8,128)(2,1)} %get-tuple-element.13.totals_in), custom_call_target="tpu_custom_call" | custom-call | tf_op jit(solution)/shard_map/pallas_call | solution.py:762

commit v7 on v6

--- a/solution.py
+++ b/solution.py
@@ -196,15 +196,14 @@
     pltpu.make_async_copy(ref, ref, sem).wait()
 
 
-def each_peer(act, first=0, last=16):
+def each_peer(act):
     def step(i, carry):
         act(16 - i)
         act(16 + i)
         return carry
 
-    if first == 0:
-        act(16)
-    lax.fori_loop(max(first, 1), last, step, 0)
+    act(16)
+    lax.fori_loop(1, 16, step, 0)
 
 
 def pack_in(d, video, cot, out):
@@ -397,11 +396,12 @@
         part = self.held.at[r, 1 - self.mine, pl.ds(i * HALF, HALF)]
         return remote(part, self.mid.at[i], self.sems["m"], 2 * r + i, self.me.at(dx=3 if i else 1))
 
-    def to_owner(self, r, i):
-        step = 3 if i else 1
+    def to_owner(self, r, i, half):
+        step, rows = (3 if i else 1), pl.ds(half * HALF, HALF)
         which = upper(wrap(self.me.x + step, 4))
         copy = remote(
-            self.held.at[r, which], self.x_in.at[i], self.sems["x"], 2 * r + i, self.me.at(dx=step)
+            self.held.at[r, which, rows], self.x_in.at[i, rows], self.sems["x"],
+            4 * r + 2 * i + half, self.me.at(dx=step),
         )
         return which, copy
 
@@ -429,23 +429,34 @@
             self.to_core(r, i).start()
 
     def core_add(self, r):
-        for i in range(2):
-            self.to_core(r, i).wait_recv()
+        def add(i):
             slot = (1 - self.me.core if r else self.me.core) + 2 * i
             both = self.sums[r, slot].astype(F32) + self.core_in[r, i].astype(F32)
             self.held[r, i] = both.astype(BF16)
 
-        def act():
+        for i in range(2):
+            self.to_core(r, i).wait_recv()
+
+        def owner():
+            add(1 - self.mine)
             for i in range(2):
                 self.to_mid(r, i).start()
-
-        self.when_owner(r, act)
+            add(self.mine)
+
+        def other():
+            for i in range(2):
+                add(i)
+            for i in range(2):
+                self.to_owner(r, i, 1 - i)[1].start()
+
+        self.when_owner(r, owner)
+        self.when_owner(1 - r, other)
 
     def relay(self, r):
         def act():
             for i in range(2):
                 self.to_mid(r, i).wait_recv()
-                which, copy = self.to_owner(r, i)
+                which, copy = self.to_owner(r, i, i)
                 rows = pl.ds(i * HALF, HALF)
                 both = self.held[r, which, rows, :].astype(F32) + self.mid[i].astype(F32)
                 self.held[r, which, rows, :] = both.astype(BF16)
@@ -457,7 +468,8 @@
         def act():
             total = self.held[r, self.mine].astype(F32)
             for i in range(2):
-                self.to_owner(r, i)[1].wait_recv()
+                for half in range(2):
+                    self.to_owner(r, i, half)[1].wait_recv()
                 total = total + self.x_in[i].astype(F32)
             self.held[r, self.mine] = total.astype(BF16)
             for k in FAR_FIRST:
@@ -498,7 +510,8 @@
 
             def other(r=r):
                 for i in range(2):
-                    self.to_owner(r, i)[1].wait_send()
+                    for half in range(2):
+                        self.to_owner(r, i, half)[1].wait_send()
 
             self.when_owner(r, owner)
             self.when_owner(1 - r, other)
@@ -675,9 +688,8 @@
     total.relay(1)
     total.own_x(0)
     total.own_x(1)
-    each_peer(lambda k: going(1, k).start(), 0, 8)
     total.own_z()
-    each_peer(lambda k: going(1, k).start(), 8, 16)
+    each_peer(lambda k: going(1, k).start())
     total.own_y()
     for part in range(2):
         returned(part, o_r)
@@ -718,7 +730,7 @@
         held(2, 4, C, C), held(2, 2, C, C), held(2, 2, C, C), held(2, HALF, C), held(2, C, C),
         held(8, QUAD, C), held(8, QUAD, C), held(QUAD, C),
     ]
-    counts = [5] + [2] * 6 + [8, 8, 2, 2, 4, 4, 8, 8] + [4] * 6 + [1] * 6
+    counts = [5] + [2] * 6 + [8, 8, 2, 2, 4, 4, 8, 8] + [4] * 4 + [8] * 2 + [1] * 6
     scratch += [pltpu.SemaphoreType.DMA((n,)) for n in counts]
     outs = [(args[0].shape, BF16), ((8, QUAD, C), BF16)]
     places = [pl.ANY] * 5 + [pltpu.VMEM]

time: 95.3 us -> 93.7 us (0.983)
  Pallas kernels: 94.3 us -> 92.7 us
    pallas_call x1, Pallas kernels: 91.9 us -> 90.3 us  [main(): call(main_kernel, outs, scratch, places, [pltpu.VMEM] * 2, 56, 1)(*args)]
where the time goes in v7:
time: 93.7 us; the launch traced here: 93.5 us
  Pallas kernels  92.7 us (99%)
    pallas_call x1, Pallas kernels, main(): call(main_kernel, outs, scratch, places, [pltpu.VMEM] * 2, 56, 1)(*args)  90.3 us
    pallas_call x1, Pallas kernels, body(): call(functools.partial(finish_kernel, factor), outs, [pltpu.VMEM(video.sh...  2.46 us

profile of v7, /device:TPU:1, one launch (start us, length us, event | category | flops | bytes accessed | tf_op | source)
XLA Modules:
  0.0 93.5 jit_solution(14185993424968741701)
XLA Ops:
  0.6 90.3 %shard_map.101 = (bf16[1,2,288,384]{3,2,1,0:T(8,128)(2,1)}, bf16[8,48,384]{2,1,0:T(8,128)(2,1)}) custom-call(bf16[1,2,288,384]{3,2,1,0:T(8,128)(2,1)} %video_in.1, bf16[1,2,288,384]{3,2,1,0:T(8,128)(2,1)} %cot_in.1, bf16[3,12,384]{2,1,0:T(8,128)(2,1)} %conv_in.1, bf16[12,1152]{1,0:T(8,128)(2,1)} %qkv_in.1, bf16[12,384]{1,0:T(8,128)(2,1)} %out_in.1, ...), custom_call_target="tpu_custom_call" | custom-call | tf_op jit(solution)/shard_map/pallas_call | solution.py:737
  90.9 2.5 %shard_map.102 = (bf16[1,2,288,384]{3,2,1,0:T(8,128)(2,1)}, f32[3,12,384]{2,1,0:T(8,128)}, f32[12,1152]{1,0:T(8,128)}, f32[12,384]{1,0:T(8,128)}, f32[1,12]{1,0:T(1,128)}) custom-call(bf16[1,2,288,384]{3,2,1,0:T(8,128)(2,1)} %get-tuple-element.12.grad_in, bf16[8,48,384]{2,1,0:T(8,128)(2,1)} %get-tuple-element.13.totals_in), custom_call_target="tpu_custom_call" | custom-call | tf_op jit(solution)/shard_map/pallas_call | solution.py:774

commit v8 on v7

--- a/solution.py
+++ b/solution.py
@@ -684,10 +684,10 @@
             conv_back(blocks, w, pgrad_hidden, pa1, pa2, pgv)
             total.core_add(1)
             total.relay(0)
-            send_back()
     total.relay(1)
     total.own_x(0)
     total.own_x(1)
+    send_back()
     total.own_z()
     each_peer(lambda k: going(1, k).start())
     total.own_y()

time: 93.7 us -> 93.7 us (level)
  no operation moved by 1% of the time
where the time goes in v8:
time: 93.7 us; the launch traced here: 93.5 us
  Pallas kernels  92.7 us (99%)
    pallas_call x1, Pallas kernels, main(): call(main_kernel, outs, scratch, places, [pltpu.VMEM] * 2, 56, 1)(*args)  90.3 us
    pallas_call x1, Pallas kernels, body(): call(functools.partial(finish_kernel, factor), outs, [pltpu.VMEM(video.sh...  2.46 us

profile of v8, /device:TPU:1, one launch (start us, length us, event | category | flops | bytes accessed | tf_op | source)
XLA Modules:
  0.0 93.5 jit_solution(17551446284985888275)
XLA Ops:
  0.6 90.3 %shard_map.101 = (bf16[1,2,288,384]{3,2,1,0:T(8,128)(2,1)}, bf16[8,48,384]{2,1,0:T(8,128)(2,1)}) custom-call(bf16[1,2,288,384]{3,2,1,0:T(8,128)(2,1)} %video_in.1, bf16[1,2,288,384]{3,2,1,0:T(8,128)(2,1)} %cot_in.1, bf16[3,12,384]{2,1,0:T(8,128)(2,1)} %conv_in.1, bf16[12,1152]{1,0:T(8,128)(2,1)} %qkv_in.1, bf16[12,384]{1,0:T(8,128)(2,1)} %out_in.1, ...), custom_call_target="tpu_custom_call" | custom-call | tf_op jit(solution)/shard_map/pallas_call | solution.py:737
  90.9 2.5 %shard_map.102 = (bf16[1,2,288,384]{3,2,1,0:T(8,128)(2,1)}, f32[3,12,384]{2,1,0:T(8,128)}, f32[12,1152]{1,0:T(8,128)}, f32[12,384]{1,0:T(8,128)}, f32[1,12]{1,0:T(1,128)}) custom-call(bf16[1,2,288,384]{3,2,1,0:T(8,128)(2,1)} %get-tuple-element.12.grad_in, bf16[8,48,384]{2,1,0:T(8,128)(2,1)} %get-tuple-element.13.totals_in), custom_call_target="tpu_custom_call" | custom-call | tf_op jit(solution)/shard_map/pallas_call | solution.py:774
